TPU v7x, 256 devices: a whole 4x4x8 slice. The times are simulated.
256 devices in a mesh: dp: 2 (over y_hi), row: 8 (over x, y_lo), col: 16 (over z, core).
Axes of the slice: x: 4, y: 4 (y_hi: 2, y_lo: 2; y = y_hi * 2 + y_lo), z: 8, core: 2. Of those that a mesh axis runs over, the one named last changes fastest.
Arguments:
- view_a: bfloat16 [256, 32768], P('dp', ('row', 'col')), may hold values from -22 to 22
- view_b: bfloat16 [256, 32768], P('dp', ('row', 'col')), may hold values from -22 to 22
Outputs:
- grad_a: float32 [256, 32768], P('dp', ('row', 'col'))
- grad_b: float32 [256, 32768], P('dp', ('row', 'col'))
- objective: float32 [], replicated
All inputs are finite; a program needn't handle non-finite values.
Results may differ from a plain program's by a relative error of at most 0.0028.
Values may be sent and summed in bfloat16 or wider, within the bound.
No kernel may reach another device: no remote copies, remote signals or barrier semaphores. Data moves between devices by JAX's collectives and lax.ppermute only.
A program may use at most 64 MiB of HBM per device.

v0:
```python
import jax
import jax.numpy as jnp
from jax import lax
from jax.sharding import PartitionSpec as P


def statistics(values, total):
    floats = values.astype(jnp.float32)
    mean = jnp.sum(floats, axis=0) / total
    diff = floats - mean
    std = jnp.sqrt(jnp.sum(diff * diff, axis=0) / (total - 1) + 0.0001)
    return (mean, std, diff.astype(jnp.bfloat16))


def on_device(view_a, view_b):
    n_dp = lax.axis_size("dp")
    n_row = lax.axis_size("row")
    n_col = lax.axis_size("col")
    dp_index = lax.axis_index("dp")
    row_index = lax.axis_index("row")
    col_index = lax.axis_index("col")
    n_dev, shard = view_a.shape
    total = n_dev * n_dp
    f_all = shard * n_row * n_col
    coef = 2.0 * total / (25.0 * (total - 1))
    row_width = shard * n_col // n_dp
    col_width = shard * n_row
    row_start = (row_index * n_col + dp_index * (n_col // n_dp)) * shard
    full_a, full_b = (
        lax.all_gather(view_a, "dp", axis=0, tiled=True),
        lax.all_gather(view_b, "dp", axis=0, tiled=True),
    )
    mean_a, std_a, cent_a = statistics(full_a, total)
    mean_b, std_b, cent_b = statistics(full_b, total)
    wide_a, wide_b = (
        lax.all_gather(cent_a, "col", axis=1, tiled=True),
        lax.all_gather(cent_b, "col", axis=1, tiled=True),
    )
    rows_a = lax.dynamic_slice_in_dim(wide_a, dp_index * row_width, row_width, 1)
    rows_b = lax.dynamic_slice_in_dim(wide_b, dp_index * row_width, row_width, 1)
    cols_a, cols_b = (
        lax.all_gather(cent_a, "row", axis=1, tiled=True),
        lax.all_gather(cent_b, "row", axis=1, tiled=True),
    )
    block = min(512, row_width)
    column_iota = jnp.arange(col_width, dtype=jnp.int32)
    col_ids = column_iota // shard * (n_col * shard) + col_index * shard + column_iota % shard

    def tile_part(rows, cols, start):
        strip = lax.dynamic_slice_in_dim(rows, start, block, 1)
        cov = lax.dot_general(
            strip, cols, (((0,), (0,)), ((), ())), preferred_element_type=jnp.float32
        ) / (total - 1)
        row_ids = row_start + start + jnp.arange(block, dtype=jnp.int32)
        off = jnp.where(row_ids[:, None] == col_ids[None, :], jnp.float32(0.0), cov)
        contrib = jnp.dot(
            strip.astype(jnp.float32),
            off,
            preferred_element_type=jnp.float32,
            precision=lax.Precision.HIGHEST,
        )
        return (contrib, jnp.sum(off * off))

    def one_block(index, carry):
        pull_a, pull_b, square = carry
        start = index * block
        contrib_a, square_a = tile_part(rows_a, cols_a, start)
        contrib_b, square_b = tile_part(rows_b, cols_b, start)
        return (pull_a + contrib_a, pull_b + contrib_b, square + square_a + square_b)

    zeros_pull = jnp.zeros((total, col_width), jnp.float32)
    pull_a, pull_b, square = lax.fori_loop(
        0, row_width // block, one_block, (zeros_pull, zeros_pull, jnp.zeros((), jnp.float32))
    )

    def arrange(pull):
        term = coef * (pull - jnp.sum(pull, axis=0) / total)
        term = term.reshape(n_dp, n_dev, n_row, shard).transpose(0, 2, 1, 3)
        return term.reshape(n_dp * n_row * n_dev, shard)

    back_a, back_b = (
        lax.psum_scatter(arrange(pull_a), ("dp", "row"), scatter_dimension=0, tiled=True),
        lax.psum_scatter(arrange(pull_b), ("dp", "row"), scatter_dimension=0, tiled=True),
    )
    own_a = view_a.astype(jnp.float32)
    own_b = view_b.astype(jnp.float32)
    gap = own_a - own_b
    hinge_a = jnp.where(
        std_a < 1.0, total * (own_a - mean_a) / (2.0 * std_a * (total - 1)), jnp.float32(0.0)
    )
    hinge_b = jnp.where(
        std_b < 1.0, total * (own_b - mean_b) / (2.0 * std_b * (total - 1)), jnp.float32(0.0)
    )
    grad_a = gap - hinge_a + back_a
    grad_b = -gap - hinge_b + back_b
    partial_loss = 25.0 * jnp.sum(gap * gap) / (total * f_all)
    partial_loss = partial_loss + 25.0 * (
        jnp.sum(jnp.maximum(1.0 - std_a, 0.0)) + jnp.sum(jnp.maximum(1.0 - std_b, 0.0))
    ) / (f_all * n_dp)
    partial_loss = partial_loss + square / f_all
    summed = lax.psum(partial_loss, ("dp", "row", "col"))
    objective = summed * total / (50.0 * f_all)
    return (grad_a, grad_b, objective)


def solution(mesh):
    in_specs = (P("dp", ("row", "col")), P("dp", ("row", "col")))
    out_specs = (P("dp", ("row", "col")), P("dp", ("row", "col")), P())
    return jax.shard_map(
        on_device, mesh=mesh, in_specs=in_specs, out_specs=out_specs, check_vma=False
    )
```

profile of v0, /device:TPU:1, one launch (start us, length us, event | category | flops | bytes accessed | tf_op | source)
XLA Modules:
  0.0 530.5 jit_solution(17969841834913159705)
XLA Ops:
  7.2 0.0 all-gather.5.cloned.1.call-start
  7.2 6.3 %all_gather.18 = bf16[256,256]{1,0:T(8,128)(2,1)S(1)} all-gather(bf16[128,256]{1,0:T(8,128)(2,1)} %param.4), channel_id=1, replica_groups=mesh['dp'=2,'row'=8,'col'=16] {'dp'}, dimensions={0}, use_global_device_ids=true | all-gather | bytes 196608 | tf_op jit(solution)/shard_map/all_gather | solution.py:30
  13.6 0.7 fusion.43
  14.3 0.0 all-gather.5.cloned.1.call-update
  14.3 0.0 all-gather.9.cloned.1.call-start
  14.4 5.5 %all_gather.21 = bf16[256,256]{1,0:T(8,128)(2,1)S(1)} all-gather(bf16[128,256]{1,0:T(8,128)(2,1)} %param.5), channel_id=1, replica_groups=mesh['dp'=2,'row'=8,'col'=16] {'dp'}, dimensions={0}, use_global_device_ids=true | all-gather | bytes 196608 | tf_op jit(solution)/shard_map/all_gather | solution.py:31
  19.9 0.7 fusion.42
  20.6 0.0 all-gather.9.cloned.1.call-update
  20.7 0.0 all-gather.7.cloned.1.call-start
  20.7 0.7 all-gather.7.cloned.1.call-update
  21.4 0.0 all-gather.11.cloned.1.call-start
  21.4 0.5 all-gather.11.cloned.1.call-update
  22.0 0.0 reduce-scatter.5.cloned.1.call-start
  22.0 37.9 %all-gather.5.cloned.1.call-done = bf16[256,4096]{1,0:T(8,128)(2,1)} async-done(((bf16[256,256]{1,0:T(8,128)(2,1)}), bf16[256,4096]{1,0:T(8,128)(2,1)}) %all-gather.5.cloned.1.call-update) | async-done | bytes 2097168 | tf_op jit(solution)/shard_map/all_gather | solution.py:36
  60.0 1.3 constant_dynamic-slice_fusion.1
  61.2 41.2 %all-gather.9.cloned.1.call-done = bf16[256,4096]{1,0:T(8,128)(2,1)} async-done(((bf16[256,256]{1,0:T(8,128)(2,1)}), bf16[256,4096]{1,0:T(8,128)(2,1)}) %all-gather.9.cloned.1.call-update) | async-done | bytes 2097168 | tf_op jit(solution)/shard_map/all_gather | solution.py:37
  102.4 2.4 constant_dynamic-slice_fusion
  104.8 38.6 %all-gather.7.cloned.1.call-done = bf16[256,2048]{1,0:T(8,128)(2,1)} async-done(((bf16[256,256]{1,0:T(8,128)(2,1)}), bf16[256,2048]{1,0:T(8,128)(2,1)}) %all-gather.7.cloned.1.call-update) | async-done | bytes 1048592 | tf_op jit(solution)/shard_map/all_gather | solution.py:42
  143.4 49.1 %all-gather.11.cloned.1.call-done = bf16[256,2048]{1,0:T(8,128)(2,1)} async-done(((bf16[256,256]{1,0:T(8,128)(2,1)}), bf16[256,2048]{1,0:T(8,128)(2,1)}) %all-gather.11.cloned.1.call-update) | async-done | bytes 1048592 | tf_op jit(solution)/shard_map/all_gather | solution.py:43
  192.5 71.5 %while.18 = (s32[]{:T(128)}, f32[256,2048]{1,0:T(8,128)S(1)}, f32[256,2048]{1,0:T(8,128)}, f32[]{:T(128)}, bf16[256,2048]{1,0:T(8,128)(2,1)S(1)}, /*index=5*/s32...) while((s32[]{:T(128)}, f32[256,2048]{1,0:T(8,128)S(1)}, ...), condition=%wide.region_6.7_spmd.clone, body=%wide.region_3.6_spmd.clone.sunk | while | flops 7534049792 | bytes 74490264 | solution.py:72
  192.5 3.9 fusion.70
  196.4 0.0 copy-start
  196.4 0.0 copy-start.4
  196.4 0.0 copy-start.7
  196.4 5.5 %fusion.72 = f32[256,2048]{1,0:T(8,128)S(1)} fusion(f32[512,2048]{1,0:T(8,128)} %fusion.70, f32[256,2048]{1,0:T(8,128)S(1)} %get-tuple-element.331, s32[2048]{0:T(1024)S(1)} %fusion.71, s32[512]{0:T(512)S(1)} %iota_add_fusion.2, pred[]{:T(512)S(6)} %compare.6, bf16[256,2048]{1,0:T(8,128)(2,1)S(1)} %get-tuple-element.348, s32[]{:T(128)S(6)} %select_n.105), kind=kOutput, calls=%fused_computation.8.clone.1 | convolution fusion | flops 3225419776 | bytes 8660997 | tf_op jit(solution)/shard_map/while/body/eval_jaxpr/dot_general | solution.py:56
  202.0 2.5 multiply_reduce_fusion.4
  204.5 3.2 fusion.73
  207.7 1.3 copy-done.2
  210.4 3.9 fusion.70
  214.3 0.0 copy-start
  214.3 0.0 copy-start.4
  214.3 0.0 copy-start.7
  214.3 5.5 %fusion.72 = f32[256,2048]{1,0:T(8,128)S(1)} fusion(f32[512,2048]{1,0:T(8,128)} %fusion.70, f32[256,2048]{1,0:T(8,128)S(1)} %get-tuple-element.331, s32[2048]{0:T(1024)S(1)} %fusion.71, s32[512]{0:T(512)S(1)} %iota_add_fusion.2, pred[]{:T(512)S(6)} %compare.6, bf16[256,2048]{1,0:T(8,128)(2,1)S(1)} %get-tuple-element.348, s32[]{:T(128)S(6)} %select_n.105), kind=kOutput, calls=%fused_computation.8.clone.1 | convolution fusion | flops 3225419776 | bytes 8660997 | tf_op jit(solution)/shard_map/while/body/eval_jaxpr/dot_general | solution.py:56
  219.9 2.5 multiply_reduce_fusion.4
  222.3 3.2 fusion.73
  225.6 1.3 copy-done.2
  228.2 3.9 fusion.70
  232.2 5.5 %fusion.72 = f32[256,2048]{1,0:T(8,128)S(1)} fusion(f32[512,2048]{1,0:T(8,128)} %fusion.70, f32[256,2048]{1,0:T(8,128)S(1)} %get-tuple-element.331, s32[2048]{0:T(1024)S(1)} %fusion.71, s32[512]{0:T(512)S(1)} %iota_add_fusion.2, pred[]{:T(512)S(6)} %compare.6, bf16[256,2048]{1,0:T(8,128)(2,1)S(1)} %get-tuple-element.348, s32[]{:T(128)S(6)} %select_n.105), kind=kOutput, calls=%fused_computation.8.clone.1 | convolution fusion | flops 3225419776 | bytes 8660997 | tf_op jit(solution)/shard_map/while/body/eval_jaxpr/dot_general | solution.py:56
  237.8 2.5 multiply_reduce_fusion.4
  240.2 0.0 copy-done.1
  240.2 3.2 fusion.73
  243.5 1.3 copy-done.2
  246.1 3.9 fusion.70
  250.1 5.5 %fusion.72 = f32[256,2048]{1,0:T(8,128)S(1)} fusion(f32[512,2048]{1,0:T(8,128)} %fusion.70, f32[256,2048]{1,0:T(8,128)S(1)} %get-tuple-element.331, s32[2048]{0:T(1024)S(1)} %fusion.71, s32[512]{0:T(512)S(1)} %iota_add_fusion.2, pred[]{:T(512)S(6)} %compare.6, bf16[256,2048]{1,0:T(8,128)(2,1)S(1)} %get-tuple-element.348, s32[]{:T(128)S(6)} %select_n.105), kind=kOutput, calls=%fused_computation.8.clone.1 | convolution fusion | flops 3225419776 | bytes 8660997 | tf_op jit(solution)/shard_map/while/body/eval_jaxpr/dot_general | solution.py:56
  255.6 2.5 multiply_reduce_fusion.4
  258.1 3.2 fusion.73
  261.3 1.3 copy-done.2
  264.0 1.7 reduce_sum.112
  265.7 0.1 reduce_sum.110
  265.8 3.4 subtract_multiply_fusion
  269.2 0.9 copy.8
  270.1 2.0 copy.6
  272.1 0.0 reduce-scatter.5.cloned.1.call-update
  272.1 0.2 reduce-scatter.3.cloned.1.call-start
  272.3 1.3 copy-done.3
  273.7 0.9 copy.7
  274.5 1.9 copy.5
  276.5 0.0 reduce-scatter.3.cloned.1.call-update
  276.5 0.6 maximum_reduce_fusion
  277.1 0.6 maximum_reduce_fusion.1
  279.0 71.9 %reduce-scatter.5.cloned.1.call-done = f32[128,256]{1,0:T(8,128)} async-done(((f32[2048,256]{1,0:T(8,128)}), f32[128,256]{1,0:T(8,128)}) %reduce-scatter.5.cloned.1.call-update) | async-done | bytes 131088 | tf_op jit(solution)/shard_map/reduce_scatter | solution.py:83
  351.0 83.8 %reduce-scatter.3.cloned.1.call-done = f32[128,256]{1,0:T(8,128)} async-done(((f32[2048,256]{1,0:T(8,128)}), f32[128,256]{1,0:T(8,128)}) %reduce-scatter.3.cloned.1.call-update) | async-done | bytes 131088 | tf_op jit(solution)/shard_map/reduce_scatter | solution.py:82
  434.7 2.3 multiply_reduce_fusion.2
  437.7 84.1 %psum.7 = f32[]{:T(128)} all-reduce(f32[]{:T(128)S(6)} %add.148), channel_id=1, replica_groups=mesh['dp'=2,'row'=8,'col'=16] {'dp','row','col'}, use_global_device_ids=true, to_apply=%region_15.16 | all-reduce | flops 1 | bytes 8 | tf_op jit(solution)/shard_map/psum | solution.py:101
  (52 shorter events, 0.3 us)
Async XLA Ops:
  7.2 52.8 %all-gather.5.cloned.1.call-start = ((), (), s32[]{:S(2)}) async-start(), calls=%async_computation.2 | async-start | bytes 2228224 | tf_op jit(solution)/shard_map/all_gather | solution.py:36
  14.3 88.1 %all-gather.9.cloned.1.call-start = ((), (), s32[]{:S(2)}) async-start(), calls=%async_computation.4 | async-start | bytes 2228224 | tf_op jit(solution)/shard_map/all_gather | solution.py:37
  20.7 122.8 %all-gather.7.cloned.1.call-start = ((), (), s32[]{:S(2)}) async-start(), calls=%async_computation.3 | async-start | bytes 1179648 | tf_op jit(solution)/shard_map/all_gather | solution.py:42
  21.4 171.1 %all-gather.11.cloned.1.call-start = ((), (), s32[]{:S(2)}) async-start(), calls=%async_computation.5 | async-start | bytes 1179648 | tf_op jit(solution)/shard_map/all_gather | solution.py:43
  22.0 329.0 %reduce-scatter.5.cloned.1.call-start = ((), (), s32[]{:S(2)}) async-start(), calls=%async_computation.7 | async-start | bytes 2228224 | tf_op jit(solution)/shard_map/reduce_scatter | solution.py:83
  196.4 5.6 %copy-start = (f32[512,2048]{1,0:T(8,128)S(1)}, f32[512,2048]{1,0:T(8,128)}, u32[]{:S(2)}) copy-start(f32[512,2048]{1,0:T(8,128)} %fusion.70) | copy-start | bytes 12582916 | tf_op jit(solution)/shard_map/while
  196.4 5.6 %copy-start.4 = (bf16[256,2048]{1,0:T(8,128)(2,1)S(1)}, bf16[256,2048]{1,0:T(8,128)(2,1)}, u32[]{:S(2)}) copy-start(bf16[256,2048]{1,0:T(8,128)(2,1)} %get-tuple-element.351) | copy-start | bytes 3145732 | tf_op jit(solution)/shard_map/while
  196.4 5.6 %copy-start.7 = (bf16[256,2048]{1,0:T(8,128)(2,1)S(1)}, bf16[256,2048]{1,0:T(8,128)(2,1)}, u32[]{:S(2)}) copy-start(bf16[256,2048]{1,0:T(8,128)(2,1)} %get-tuple-element.352) | copy-start | bytes 3145732 | tf_op jit(solution)/shard_map/while
  202.0 2.5 copy-start.1
  207.7 1.3 copy-start.2
  214.3 5.6 %copy-start = (f32[512,2048]{1,0:T(8,128)S(1)}, f32[512,2048]{1,0:T(8,128)}, u32[]{:S(2)}) copy-start(f32[512,2048]{1,0:T(8,128)} %fusion.70) | copy-start | bytes 12582916 | tf_op jit(solution)/shard_map/while
  214.3 5.6 %copy-start.4 = (bf16[256,2048]{1,0:T(8,128)(2,1)S(1)}, bf16[256,2048]{1,0:T(8,128)(2,1)}, u32[]{:S(2)}) copy-start(bf16[256,2048]{1,0:T(8,128)(2,1)} %get-tuple-element.351) | copy-start | bytes 3145732 | tf_op jit(solution)/shard_map/while
  214.3 5.6 %copy-start.7 = (bf16[256,2048]{1,0:T(8,128)(2,1)S(1)}, bf16[256,2048]{1,0:T(8,128)(2,1)}, u32[]{:S(2)}) copy-start(bf16[256,2048]{1,0:T(8,128)(2,1)} %get-tuple-element.352) | copy-start | bytes 3145732 | tf_op jit(solution)/shard_map/while
  219.9 2.5 copy-start.1
  225.6 1.3 copy-start.2
  232.2 5.6 %copy-start = (f32[512,2048]{1,0:T(8,128)S(1)}, f32[512,2048]{1,0:T(8,128)}, u32[]{:S(2)}) copy-start(f32[512,2048]{1,0:T(8,128)} %fusion.70) | copy-start | bytes 12582916 | tf_op jit(solution)/shard_map/while
  232.2 5.6 %copy-start.4 = (bf16[256,2048]{1,0:T(8,128)(2,1)S(1)}, bf16[256,2048]{1,0:T(8,128)(2,1)}, u32[]{:S(2)}) copy-start(bf16[256,2048]{1,0:T(8,128)(2,1)} %get-tuple-element.351) | copy-start | bytes 3145732 | tf_op jit(solution)/shard_map/while
  232.2 5.6 %copy-start.7 = (bf16[256,2048]{1,0:T(8,128)(2,1)S(1)}, bf16[256,2048]{1,0:T(8,128)(2,1)}, u32[]{:S(2)}) copy-start(bf16[256,2048]{1,0:T(8,128)(2,1)} %get-tuple-element.352) | copy-start | bytes 3145732 | tf_op jit(solution)/shard_map/while
  237.7 2.5 copy-start.1
  243.5 1.3 copy-start.2
  250.0 5.6 %copy-start = (f32[512,2048]{1,0:T(8,128)S(1)}, f32[512,2048]{1,0:T(8,128)}, u32[]{:S(2)}) copy-start(f32[512,2048]{1,0:T(8,128)} %fusion.70) | copy-start | bytes 12582916 | tf_op jit(solution)/shard_map/while
  250.0 5.6 %copy-start.4 = (bf16[256,2048]{1,0:T(8,128)(2,1)S(1)}, bf16[256,2048]{1,0:T(8,128)(2,1)}, u32[]{:S(2)}) copy-start(bf16[256,2048]{1,0:T(8,128)(2,1)} %get-tuple-element.351) | copy-start | bytes 3145732 | tf_op jit(solution)/shard_map/while
  250.1 5.6 %copy-start.7 = (bf16[256,2048]{1,0:T(8,128)(2,1)S(1)}, bf16[256,2048]{1,0:T(8,128)(2,1)}, u32[]{:S(2)}) copy-start(bf16[256,2048]{1,0:T(8,128)(2,1)} %get-tuple-element.352) | copy-start | bytes 3145732 | tf_op jit(solution)/shard_map/while
  255.6 2.5 copy-start.1
  261.3 1.3 copy-start.2
  272.1 1.6 copy-start.3
  272.1 162.6 %reduce-scatter.3.cloned.1.call-start = ((), (), s32[]{:S(2)}) async-start(), calls=%async_computation.6 | async-start | bytes 2228224 | tf_op jit(solution)/shard_map/reduce_scatter | solution.py:82
  276.5 158.3 %copy-start.5 = (bf16[128,256]{1,0:T(8,128)(2,1)S(1)}, bf16[128,256]{1,0:T(8,128)(2,1)}, u32[]{:S(2)}) copy-start(bf16[128,256]{1,0:T(8,128)(2,1)} %param.5) | copy-start | bytes 196612
  276.5 158.3 %copy-start.6 = (bf16[128,256]{1,0:T(8,128)(2,1)S(1)}, bf16[128,256]{1,0:T(8,128)(2,1)}, u32[]{:S(2)}) copy-start(bf16[128,256]{1,0:T(8,128)(2,1)} %param.4) | copy-start | bytes 196612
Sparse Core Ops, SparseCore 0:
  14.4 45.4 all-gather.4
  62.3 40.0 all-gather.8
  104.7 38.6 all-gather.6
  145.6 46.8 all-gather.10
  272.2 78.6 reduce-scatter.4
  353.3 81.3 reduce-scatter.2
where the time goes:
time: 531 us; the launch traced here: 530 us
  waiting for transfers between devices  324 us (61%)
  blocking collectives  96 us (18%)
  matrix products  60.5 us (11%)
  between operations  17.9 us (3%)
  local copies, waits for them, and re-layouts  16 us (3%)
  other arithmetic  10.4 us (2%)
  loops' own time  5.61 us (1%)
    psum x1, blocking collectives, on_device(): summed = lax.psum(partial_loss, ('dp', 'row', 'col'))  84.1 us
    reduce_scatter x1, waiting for transfers between devices, on_device(): lax.psum_scatter(arrange(pull_a), ('dp', 'row'), scatter_dimension=0, til...  83.8 us
    reduce_scatter x1, waiting for transfers between devices, on_device(): lax.psum_scatter(arrange(pull_b), ('dp', 'row'), scatter_dimension=0, til...  71.9 us
    all_gather x1, waiting for transfers between devices, on_device(): lax.all_gather(cent_b, 'row', axis=1, tiled=True)  49.1 us
    all_gather x1, waiting for transfers between devices, on_device(): lax.all_gather(cent_b, 'col', axis=1, tiled=True)  41.2 us
    all_gather x1, waiting for transfers between devices, on_device(): lax.all_gather(cent_a, 'row', axis=1, tiled=True)  38.6 us
    all_gather x1, waiting for transfers between devices, on_device(): lax.all_gather(cent_a, 'col', axis=1, tiled=True)  37.9 us
    dot_general x8, matrix products, tile_part(): jnp.dot(strip.astype(jnp.float32), off, preferred_element_type=jnp.float3...  35 us
  transfers between devices with their start and end apart: 6, of which 6 were waited for; matrix products, arithmetic and copies ran while one was open for 2% of the time, Pallas kernels for 0%

commit v1 on v0

v1 whole, which is shorter than its diff:
```python
import jax
import jax.numpy as jnp
from jax import lax
from jax.experimental import pallas as pl
from jax.experimental.pallas import tpu as pltpu
from jax.sharding import Mesh, PartitionSpec as P

AXES = ("dp", "x", "yl", "z", "core")
CHIPS = ("x", "yl", "z")
TILE_R, TILE_C = 8, 128


def split3(value):
    first = value.astype(jnp.bfloat16)
    rest = value - first.astype(jnp.float32)
    second = rest.astype(jnp.bfloat16)
    third = (rest - second.astype(jnp.float32)).astype(jnp.bfloat16)
    return (first, second, third)


def place(tile, row, col, scalar):
    rows = lax.broadcasted_iota(jnp.int32, tile.shape, 0)
    cols = lax.broadcasted_iota(jnp.int32, tile.shape, 1)
    return jnp.where((rows == row) & (cols == col), scalar, tile)


def pick(tile, row, col):
    rows = lax.broadcasted_iota(jnp.int32, tile.shape, 0)
    cols = lax.broadcasted_iota(jnp.int32, tile.shape, 1)
    kept = jnp.where((rows == row) & (cols == col), tile, jnp.float32(0.0))
    return jnp.sum(kept, axis=(0, 1), keepdims=True)


def total_sum(value):
    return jnp.sum(value, axis=(0, 1), keepdims=True)


def gram_kernel(n_all, f_all, own_a, own_b, far, tiles, cent_a, cent_b, base_a, base_b):
    n_dev = own_a.shape[0]
    coef = 2.0 * n_all / (25.0 * (n_all - 1))
    near = (own_a[...].astype(jnp.float32), own_b[...].astype(jnp.float32))
    other = (far[0].astype(jnp.float32), far[1].astype(jnp.float32))
    gap = near[0] - near[1]
    gap_far = other[0] - other[1]
    common = (25.0 / (n_all * f_all)) * (total_sum(gap * gap) + total_sum(gap_far * gap_far))
    grams = []
    for view, (cent, base) in enumerate(((cent_a, base_a), (cent_b, base_b))):
        mine, theirs = near[view], other[view]
        mean = (
            jnp.sum(mine, axis=0, keepdims=True) + jnp.sum(theirs, axis=0, keepdims=True)
        ) / n_all
        diff, diff_far = mine - mean, theirs - mean
        squares = jnp.sum(diff * diff, axis=0, keepdims=True) + jnp.sum(
            diff_far * diff_far, axis=0, keepdims=True
        )
        std = jnp.sqrt(squares / (n_all - 1) + 0.0001)
        c_near, c_far = diff.astype(jnp.bfloat16), diff_far.astype(jnp.bfloat16)
        cent[:n_dev] = c_near
        cent[n_dev:] = c_far
        f_near, f_far = c_near.astype(jnp.float32), c_far.astype(jnp.float32)
        r = jnp.sum(f_near, axis=0, keepdims=True) + jnp.sum(f_far, axis=0, keepdims=True)
        d = (
            jnp.sum(f_near * f_near, axis=0, keepdims=True)
            + jnp.sum(f_far * f_far, axis=0, keepdims=True)
        ) / (n_all - 1)
        hinge = jnp.where(std < 1.0, n_all / (2.0 * std * (n_all - 1)), jnp.float32(0.0))
        sign = 1.0 if view == 0 else -1.0
        base[...] = sign * gap - hinge * diff - coef * (d * (f_near - r / n_all))
        common = common + (25.0 / f_all) * total_sum(jnp.maximum(1.0 - std, 0.0))
        common = common - total_sum(d * d) / f_all
        every = jnp.concatenate([c_near, c_far], axis=0)
        dims = (((1,), (1,)), ((), ()))
        r1, r2, r3 = split3(r)
        rows16 = lax.broadcasted_iota(jnp.int32, (16, r.shape[1]), 0)
        zero = jnp.zeros((), jnp.float32)
        r_rows = jnp.where(
            rows16 == 0,
            r1.astype(jnp.float32),
            jnp.where(
                rows16 == 1,
                r2.astype(jnp.float32),
                jnp.where(rows16 == 2, r3.astype(jnp.float32), zero),
            ),
        ).astype(jnp.bfloat16)
        gram = lax.dot_general(c_near, every, dims, preferred_element_type=jnp.float32)
        v_rows = lax.dot_general(r_rows, every, dims, preferred_element_type=jnp.float32)
        v = jnp.sum(v_rows, axis=0, keepdims=True)
        grams.append((gram - v / n_all, total_sum(r * r)))
    per_view = tiles.shape[0] // 2
    for view, (gram, s) in enumerate(grams):
        for i in range(per_view):
            rt, lt = i // 2, i % 2
            tile = gram[rt * TILE_R : (rt + 1) * TILE_R, lt * TILE_C : (lt + 1) * TILE_C]
            if i == 0:
                tile = place(tile, 1, 0, s)
                if view == 0:
                    tile = place(tile, 3, 2, common)
            tiles[view * per_view + i] = tile


def final_kernel(n_all, f_all, tiles, cent_a, cent_b, base_a, base_b, grad_a, grad_b, part):
    n_dev = base_a.shape[0]
    coef = 2.0 * n_all / (25.0 * (n_all - 1))
    per_view = tiles.shape[0] // 2
    square = jnp.zeros((1, 1), jnp.float32)
    common = jnp.zeros((1, 1), jnp.float32)
    for view, (cent, base, grad) in enumerate(
        ((cent_a, base_a, grad_a), (cent_b, base_b, grad_b))
    ):
        rows = []
        for rt in range(per_view // 2):
            left, right = tiles[view * per_view + 2 * rt], tiles[view * per_view + 2 * rt + 1]
            rows.append(jnp.concatenate([left, right], axis=1))
        top = rows[0]
        s = pick(top, 1, 0)
        zero = jnp.float32(0.0)
        top = place(top, 1, 0, zero)
        if view == 0:
            common = common + pick(top, 3, 2)
            top = place(top, 3, 2, zero)
        sums = jnp.sum(top, axis=1, keepdims=True)

        def recover(row, col):
            delta = (sums[row : row + 1] - sums[col : col + 1]) / n_all
            return (pick(top, col, row) + delta) / (1.0 - 1.0 / n_all)

        fixed = place(top, 1, 0, recover(1, 0))
        if view == 0:
            fixed = place(fixed, 3, 2, recover(3, 2))
        rows[0] = fixed
        gram = jnp.concatenate(rows, axis=0)
        row_sums = jnp.sum(gram, axis=1, keepdims=True)
        square = square + total_sum(gram * gram) + total_sum(row_sums * row_sums) / n_all
        square = square + 0.5 * s * s / (n_all * n_all)
        parts = jnp.concatenate(split3(gram), axis=0)
        pulls = jnp.dot(parts, cent[...], preferred_element_type=jnp.float32)
        pull = pulls[:n_dev] + pulls[n_dev : 2 * n_dev] + pulls[2 * n_dev :]
        grad[...] = base[...] + (coef / (n_all - 1)) * pull
    loss = 0.5 * common + square / (float(n_all - 1) * float(n_all - 1) * f_all)
    part[...] = jnp.broadcast_to(loss * n_all / (50.0 * f_all), part.shape)


def on_device(view_a, view_b):
    n_dp = lax.axis_size("dp")
    n_chips = lax.axis_size(CHIPS)
    n_dev, shard = view_a.shape
    n_all = n_dev * n_dp
    f_all = shard * n_chips * lax.axis_size("core")
    swap = [(0, 1), (1, 0)]
    vmem = pl.BlockSpec(memory_space=pltpu.VMEM)
    far = lax.ppermute(jnp.stack([view_a, view_b]), "dp", swap)
    f32, bf16 = jnp.float32, jnp.bfloat16
    n_tiles = 2 * n_dev * n_all // (TILE_R * TILE_C)
    tiles, cent_a, cent_b, base_a, base_b = pl.pallas_call(
        lambda *refs: gram_kernel(n_all, f_all, *refs),
        out_shape=(
            jax.ShapeDtypeStruct((n_tiles, TILE_R, TILE_C), f32),
            jax.ShapeDtypeStruct((n_all, shard), bf16),
            jax.ShapeDtypeStruct((n_all, shard), bf16),
            jax.ShapeDtypeStruct((n_dev, shard), f32),
            jax.ShapeDtypeStruct((n_dev, shard), f32),
        ),
        in_specs=[vmem] * 3,
        out_specs=(vmem,) * 5,
        compiler_params=pltpu.CompilerParams(vmem_limit_bytes=32 * 1024 * 1024),
        name="gram",
    )(view_a, view_b, far)
    shares = lax.all_to_all(tiles, CHIPS, 0, 0, tiled=True)
    share = jnp.sum(shares.reshape(n_chips, n_tiles // n_chips, TILE_R, TILE_C), axis=0)
    share = share + lax.ppermute(share, "core", swap)
    spread = jnp.broadcast_to(share[None], (n_chips,) + share.shape)
    whole = lax.all_to_all(spread.reshape(tiles.shape), CHIPS, 0, 0, tiled=True)
    grad_a, grad_b, part = pl.pallas_call(
        lambda *refs: final_kernel(n_all, f_all, *refs),
        out_shape=(
            jax.ShapeDtypeStruct((n_dev, shard), f32),
            jax.ShapeDtypeStruct((n_dev, shard), f32),
            jax.ShapeDtypeStruct((TILE_R, TILE_C), f32),
        ),
        in_specs=[vmem] * 5,
        out_specs=(vmem,) * 3,
        compiler_params=pltpu.CompilerParams(vmem_limit_bytes=32 * 1024 * 1024),
        name="final",
    )(whole, cent_a, cent_b, base_a, base_b)
    objective = part[0, 0] + lax.ppermute(part, "dp", swap)[0, 0]
    return (grad_a, grad_b, objective)


def solution(mesh):
    fine = Mesh(mesh.devices.reshape(2, 4, 2, 8, 2), AXES)
    spec = P("dp", ("x", "yl", "z", "core"))
    return jax.shard_map(
        on_device, mesh=fine, in_specs=(spec, spec), out_specs=(spec, spec, P()), check_vma=False
    )
```

time: 531 us -> 63.2 us (0.12)
  the two profiles are of different devices: /device:TPU:1 before, /device:TPU:16 now
where the time goes in v1:
time: 63.2 us; the launch traced here: 63 us
  blocking collectives  43.4 us (69%)
  waiting for transfers between devices  9.79 us (15%)
  between operations  3.07 us (5%)
  starting transfers between devices  2.87 us (5%)
  Pallas kernels  1.82 us (3%)
  local copies, waits for them, and re-layouts  1.06 us (2%)
  other arithmetic  0.99 us (2%)
    all_to_all x1, blocking collectives, on_device(): shares = lax.all_to_all(tiles, CHIPS, 0, 0, tiled=True)  25.2 us
    all_to_all x1, blocking collectives, on_device(): whole = lax.all_to_all(spread.reshape(tiles.shape), CHIPS, 0, 0, tiled=True)  18.2 us
    ppermute x1, waiting for transfers between devices, on_device(): far = lax.ppermute(jnp.stack([view_a, view_b]), 'dp', swap)  4.67 us
    ppermute x1, waiting for transfers between devices, on_device(): objective = part[0, 0] + lax.ppermute(part, 'dp', swap)[0, 0]  3.97 us
    ppermute x1, starting transfers between devices, on_device(): far = lax.ppermute(jnp.stack([view_a, view_b]), 'dp', swap)  2.16 us
    pallas_call x1, Pallas kernels, on_device(): pl.pallas_call(lambda *refs: final_kernel(n_all, f_all, *refs), out_shape...  1.32 us
  transfers between devices with their start and end apart: 3, of which 3 were waited for; matrix products, arithmetic and copies ran while one was open for 1% of the time, Pallas kernels for 0%

profile of v1, /device:TPU:16, one launch (start us, length us, event | category | flops | bytes accessed | tf_op | source)
XLA Modules:
  0.0 63.0 jit_solution(7459563819140997970)
XLA Ops:
  0.6 0.0 copy-start
  0.6 0.0 copy-start.1
  0.7 0.9 %pad_maximum_fusion = bf16[2,128,256]{2,1,0:T(8,128)(2,1)S(1)} fusion(bf16[1,128,256]{2,1,0:T(8,128)(2,1)} %bitcast.8, bf16[1,128,256]{2,1,0:T(8,128)(2,1)} %bitcast.7), kind=kLoop, calls=%fused_computation | loop fusion | flops 65536 | bytes 262144 | tf_op jit(solution)/shard_map/stack | solution.py:151
  1.6 2.2 %collective-permute-start = (bf16[2,128,256]{2,1,0:T(8,128)(2,1)S(1)}, bf16[2,128,256]{2,1,0:T(8,128)(2,1)S(1)}, u32[]{:S(2)}, u32[]{:S(2)}) collective-permute-start(bf16[2,128,256]{2,1,0:T(8,128)(2,1)S(1)} %pad_maximum_fusion), channel_id=1, source_target_pairs={{0,128},{128,0},{1,129},{129,1},{2,130},{130,2},{3,131},{131,3},{4... | collective-permute-start | bytes 393224 | tf_op jit(solution)/shard_map/ppermute | solution.py:151
  3.7 4.7 %collective-permute-done.refs_2_ = bf16[2,128,256]{2,1,0:T(8,128)(2,1)S(1)} collective-permute-done((bf16[2,128,256]{2,1,0:T(8,128)(2,1)S(1)}, bf16[2,128,256]{2,1,0:T(8,128)(2,1)S(1)}, u32[]{:S(2)}, u32[]{:S(2)}) %collective-permute-start) | collective-permute-done | bytes 131104 | tf_op jit(solution)/shard_map/ppermute | solution.py:151
  8.4 0.0 copy-done
  8.4 0.0 copy-done.1
  8.4 0.5 gram.1
  8.9 25.2 %all_to_all.10 = f32[64,8,128]{2,1,0:T(8,128)S(1)} all-to-all(f32[64,8,128]{2,1,0:T(8,128)S(1)} %get-tuple-element.11), channel_id=1, replica_groups=mesh['dp'=2,'x'=4,'yl'=2,'z'=8,'core'=2] {'x','yl','z'}, dimensions={0} | all-to-all | bytes 524288 | tf_op jit(solution)/shard_map/all_to_all | solution.py:168
  34.1 0.1 reduce_sum.11
  34.1 0.1 collective-permute-start.1
  34.2 1.2 %collective-permute-done.1 = f32[1,8,128]{2,1,0:T(8,128)S(1)} collective-permute-done((f32[1,8,128]{2,1,0:T(8,128)S(1)}, f32[1,8,128]{2,1,0:T(8,128)S(1)}, u32[]{:S(2)}, u32[]{:S(2)}) %collective-permute-start.1) | collective-permute-done | bytes 4128 | tf_op jit(solution)/shard_map/ppermute | solution.py:170
  35.4 18.2 %all_to_all.11.refs_0_ = f32[64,8,128]{2,1,0:T(8,128)S(1)} all-to-all(f32[64,8,128]{2,1,0:T(8,128)S(1)} %reshape.15), channel_id=1, replica_groups=mesh['dp'=2,'x'=4,'yl'=2,'z'=8,'core'=2] {'x','yl','z'}, dimensions={0} | all-to-all | bytes 524288 | tf_op jit(solution)/shard_map/all_to_all | solution.py:172
  53.7 1.3 %final.1 = (f32[128,256]{1,0:T(8,128)}, f32[128,256]{1,0:T(8,128)}, f32[8,128]{1,0:T(8,128)S(1)}) custom-call(f32[64,8,128]{2,1,0:T(8,128)S(1)} %all_to_all.11.refs_0_, bf16[256,256]{1,0:T(8,128)(2,1)S(1)} %get-tuple-element.12.refs_1_, bf16[256,256]{1,0:T(8,128)(2,1)S(1)} %get-tuple-element.13.refs_2_, f32[128,256]{1,0:T(8,128)S(1)} %get-tuple-element.14.refs_3_, ...), custom_call_target="tpu_custom_call" | custom-call | tf_op jit(solution)/shard_map/final/pallas_call | solution.py:173
  55.0 0.6 collective-permute-start.2
  55.6 0.5 slice.6
  56.1 4.0 %collective-permute-done.2 = f32[8,128]{1,0:T(8,128)S(1)} collective-permute-done((f32[8,128]{1,0:T(8,128)S(1)}, f32[8,128]{1,0:T(8,128)S(1)}, u32[]{:S(2)}, u32[]{:S(2)}) %collective-permute-start.2) | collective-permute-done | bytes 4128 | tf_op jit(solution)/shard_map/ppermute | solution.py:185
  60.1 0.5 slice.7
  (2 shorter events, 0.0 us)
Async XLA Ops:
  0.6 7.8 %copy-start = (bf16[128,256]{1,0:T(8,128)(2,1)S(1)}, bf16[128,256]{1,0:T(8,128)(2,1)}, u32[]{:S(2)}) copy-start(bf16[128,256]{1,0:T(8,128)(2,1)} %refs_0_.1) | copy-start | bytes 196612
  0.6 7.8 %copy-start.1 = (bf16[128,256]{1,0:T(8,128)(2,1)S(1)}, bf16[128,256]{1,0:T(8,128)(2,1)}, u32[]{:S(2)}) copy-start(bf16[128,256]{1,0:T(8,128)(2,1)} %refs_1_.1) | copy-start | bytes 196612
  1.6 6.8 %collective-permute-start = (bf16[2,128,256]{2,1,0:T(8,128)(2,1)S(1)}, bf16[2,128,256]{2,1,0:T(8,128)(2,1)S(1)}, u32[]{:S(2)}, u32[]{:S(2)}) collective-permute-start(bf16[2,128,256]{2,1,0:T(8,128)(2,1)S(1)} %pad_maximum_fusion), channel_id=1, source_target_pairs={{0,128},{128,0},{1,129},{129,1},{2,130},{130,2},{3,131},{131,3},{4... | collective-permute-start | bytes 393224 | tf_op jit(solution)/shard_map/ppermute | solution.py:151
  34.1 1.2 %collective-permute-start.1 = (f32[1,8,128]{2,1,0:T(8,128)S(1)}, f32[1,8,128]{2,1,0:T(8,128)S(1)}, u32[]{:S(2)}, u32[]{:S(2)}) collective-permute-start(f32[1,8,128]{2,1,0:T(8,128)S(1)} %bitcast.9), channel_id=1, source_target_pairs={{0,1},{1,0},{2,3},{3,2},{4,5},{5,4},{6,7},{7,6},{8,9},{9,8},{10,11... | collective-permute-start | bytes 12296 | tf_op jit(solution)/shard_map/ppermute | solution.py:170
  55.0 5.1 %collective-permute-start.2 = (f32[8,128]{1,0:T(8,128)S(1)}, f32[8,128]{1,0:T(8,128)S(1)}, u32[]{:S(2)}, u32[]{:S(2)}) collective-permute-start(f32[8,128]{1,0:T(8,128)S(1)} %get-tuple-element.18), channel_id=1, source_target_pairs={{0,128},{128,0},{1,129},{129,1},{2,130},{130,2},{3,131},{131,3},{4... | collective-permute-start | bytes 12296 | tf_op jit(solution)/shard_map/ppermute | solution.py:185

commit v2 on v0

v2 whole, which is shorter than its diff:
```python
import jax
import jax.numpy as jnp
from jax import lax
from jax.experimental import pallas as pl
from jax.experimental.pallas import tpu as pltpu
from jax.sharding import Mesh, PartitionSpec as P

AXES = ("dp", "x", "yl", "z", "core")
CHIPS = ("x", "yl", "z")
PIECES = 5
F32, BF16 = jnp.float32, jnp.bfloat16
ROW_DIMS = (((1,), (1,)), ((), ()))


def split3(value):
    first = value.astype(BF16)
    rest = value - first.astype(F32)
    second = rest.astype(BF16)
    third = (rest - second.astype(F32)).astype(BF16)
    return (first, second, third)


def iotas(shape):
    return (lax.broadcasted_iota(jnp.int32, shape, 0), lax.broadcasted_iota(jnp.int32, shape, 1))


def total_sum(value):
    return jnp.sum(value, axis=(0, 1), keepdims=True)


def col_sum(value):
    return jnp.sum(value, axis=0, keepdims=True)


def pack(gram, scalar):
    g00, g01, g11 = gram
    n = g00.shape[0]
    rows, cols = iotas(g00.shape)
    both = jnp.where(rows < cols, g00, g11)
    diag = col_sum(jnp.where(rows == cols, g00, F32(0.0)))
    erows, ecols = iotas((n // 2, n))
    extra = jnp.where(erows == 0, diag, F32(0.0))
    extra = jnp.where((erows == 1) & (ecols == 0), scalar, extra)
    return (both[: n // 2], both[n // 2 :], g01[: n // 2], g01[n // 2 :], extra)


def unpack(pieces):
    both = jnp.concatenate([pieces[0], pieces[1]], axis=0)
    g01 = jnp.concatenate([pieces[2], pieces[3]], axis=0)
    extra = pieces[4]
    rows, cols = iotas(both.shape)
    zero = F32(0.0)
    upper = jnp.where(rows < cols, both, zero)
    lower = jnp.where(rows > cols, both, zero)
    on_diag = rows == cols
    g00 = upper + upper.T + jnp.where(on_diag, extra[0:1], zero)
    g11 = lower + lower.T + jnp.where(on_diag, both, zero)
    return ((g00, g01, g11), extra[1:2, 0:1])


def store_pieces(ref, pieces):
    for j, piece in enumerate(pieces):
        ref[pl.ds(j, piece.shape[0], stride=PIECES), :] = piece


def load_pieces(ref):
    count = ref.shape[0] // PIECES
    return [ref[pl.ds(j, count, stride=PIECES), :] for j in range(PIECES)]


def gram_kernel(n_all, f_all, place, near, far, keep, send, cent, base):
    n_dev = near.shape[1]
    coef = 2.0 * n_all / (25.0 * (n_all - 1))
    first_plane = place[0] == 0
    first_core = place[1] == 0
    views = []
    for view in range(2):
        mine, theirs = near[view].astype(F32), far[view].astype(F32)
        views.append((jnp.where(first_plane, mine, theirs), jnp.where(first_plane, theirs, mine)))
    gap0 = views[0][0] - views[1][0]
    gap1 = views[0][1] - views[1][1]
    gap = jnp.where(first_plane, gap0, gap1)
    packed = []
    for view, (z0, z1) in enumerate(views):
        mean = (col_sum(z0) + col_sum(z1)) / n_all
        diff0, diff1 = z0 - mean, z1 - mean
        squares = col_sum(diff0 * diff0) + col_sum(diff1 * diff1)
        std = jnp.sqrt(squares / (n_all - 1) + 0.0001)
        c0, c1 = diff0.astype(BF16), diff1.astype(BF16)
        cent[view, :n_dev] = c0
        cent[view, n_dev:] = c1
        f0, f1 = c0.astype(F32), c1.astype(F32)
        r = col_sum(f0) + col_sum(f1)
        d = (col_sum(f0 * f0) + col_sum(f1 * f1)) / (n_all - 1)
        hinge = jnp.where(std < 1.0, n_all / (2.0 * std * (n_all - 1)), F32(0.0))
        diff = jnp.where(first_plane, diff0, diff1)
        own = jnp.where(first_plane, f0, f1)
        sign = 1.0 if view == 0 else -1.0
        base[view] = sign * gap - hinge * diff - coef * (d * (own - r / n_all))
        scalar = (25.0 / f_all) * total_sum(jnp.maximum(1.0 - std, 0.0)) - total_sum(d * d) / f_all
        if view == 0:
            squared_gap = total_sum(gap0 * gap0) + total_sum(gap1 * gap1)
            scalar = scalar + (25.0 / (n_all * f_all)) * squared_gap
        every = jnp.concatenate([c0, c1], axis=0)
        top = lax.dot_general(c0, every, ROW_DIMS, preferred_element_type=F32)
        low = lax.dot_general(c1, c1, ROW_DIMS, preferred_element_type=F32)
        packed.append(pack((top[:, :n_dev], top[:, n_dev:], low), scalar))
    store_pieces(keep, [jnp.where(first_core, a, b) for a, b in zip(*packed)])
    store_pieces(send, [jnp.where(first_core, b, a) for a, b in zip(*packed)])


def share_kernel(shares, spread):
    for j, piece in enumerate(load_pieces(shares)):
        spread[pl.ds(j, piece.shape[0], stride=PIECES), :] = jnp.broadcast_to(
            col_sum(piece), piece.shape
        )


def final_kernel(n_all, f_all, place, mine, theirs, cent, base, grad_a, grad_b, objective):
    n_dev = base.shape[1]
    coef = 2.0 * n_all / (25.0 * (n_all - 1))
    first_plane = place[0] == 0
    first_core = place[1] == 0
    mine_pieces, theirs_pieces = load_pieces(mine), load_pieces(theirs)
    square = jnp.zeros((1, 1), F32)
    loss = jnp.zeros((1, 1), F32)
    for view, grad in enumerate((grad_a, grad_b)):
        mine_here = first_core if view == 0 else jnp.logical_not(first_core)
        pieces = [jnp.where(mine_here, m, t) for m, t in zip(mine_pieces, theirs_pieces)]
        (g00, g01, g11), scalar = unpack(pieces)
        g10 = g01.T
        loss = loss + scalar
        square = square + total_sum(g00 * g00 + 2.0 * (g01 * g01) + g11 * g11)
        v0 = col_sum(g00) + col_sum(g10)
        v1 = col_sum(g01) + col_sum(g11)
        left = jnp.where(first_plane, g00, g10) - v0 / n_all
        right = jnp.where(first_plane, g01, g11) - v1 / n_all
        rows = jnp.concatenate([left, right], axis=1)
        parts = jnp.concatenate(split3(rows), axis=0)
        pulls = jnp.dot(parts, cent[view], preferred_element_type=F32)
        pull = pulls[:n_dev] + pulls[n_dev : 2 * n_dev] + pulls[2 * n_dev :]
        grad[...] = base[view] + (coef / (n_all - 1)) * pull
    loss = loss + square / (float(n_all - 1) * float(n_all - 1) * f_all)
    objective[...] = loss * n_all / (50.0 * f_all)


def on_device(view_a, view_b):
    n_dp = lax.axis_size("dp")
    n_chips = lax.axis_size(CHIPS)
    n_dev, shard = view_a.shape
    n_all = n_dev * n_dp
    f_all = shard * n_chips * lax.axis_size("core")
    swap = [(0, 1), (1, 0)]
    vmem = pl.BlockSpec(memory_space=pltpu.VMEM)
    smem = pl.BlockSpec(memory_space=pltpu.SMEM)
    params = pltpu.CompilerParams(vmem_limit_bytes=32 * 1024 * 1024)
    place = jnp.stack([lax.axis_index("dp"), lax.axis_index("core")]).astype(jnp.int32)
    near = jnp.stack([view_a, view_b])
    far = lax.ppermute(near, "dp", swap)
    half = n_dev // 2
    packed = jax.ShapeDtypeStruct((PIECES * half, n_dev), F32)
    keep, send, cent, base = pl.pallas_call(
        lambda *refs: gram_kernel(n_all, f_all, *refs),
        out_shape=(
            packed,
            packed,
            jax.ShapeDtypeStruct((2, n_all, shard), BF16),
            jax.ShapeDtypeStruct((2, n_dev, shard), F32),
        ),
        in_specs=[smem, vmem, vmem],
        out_specs=(vmem,) * 4,
        compiler_params=params,
        name="gram",
    )(place, near, far)

    def exchange(rows):
        chunks = rows.reshape(n_chips, 1, PIECES * half * n_dev // n_chips)
        moved = lax.all_to_all(chunks, CHIPS, 0, 0, tiled=True)
        return moved.reshape(rows.shape)

    chip_sum = keep + lax.ppermute(send, "core", swap)
    shares = exchange(chip_sum)
    spread = pl.pallas_call(
        share_kernel,
        out_shape=packed,
        in_specs=[vmem],
        out_specs=vmem,
        compiler_params=params,
        name="share",
    )(shares)
    mine = exchange(spread)
    theirs = lax.ppermute(mine, "core", swap)
    grad_a, grad_b, objective = pl.pallas_call(
        lambda *refs: final_kernel(n_all, f_all, *refs),
        out_shape=(
            jax.ShapeDtypeStruct((n_dev, shard), F32),
            jax.ShapeDtypeStruct((n_dev, shard), F32),
            jax.ShapeDtypeStruct((1, 1), F32),
        ),
        in_specs=[smem] + [vmem] * 4,
        out_specs=(vmem,) * 3,
        compiler_params=params,
        name="final",
    )(place, mine, theirs, cent, base)
    return (grad_a, grad_b, objective.reshape(()))


def solution(mesh):
    fine = Mesh(mesh.devices.reshape(2, 4, 2, 8, 2), AXES)
    spec = P("dp", ("x", "yl", "z", "core"))
    return jax.shard_map(
        on_device, mesh=fine, in_specs=(spec, spec), out_specs=(spec, spec, P()), check_vma=False
    )
```

time: 531 us -> 55.7 us (0.10)
  waiting for transfers between devices: 324 us -> 4.34 us
  matrix products: 60.5 us -> 0 us
  blocking collectives: 96 us -> 36.7 us
  between operations: 17.9 us -> 0.65 us
  local copies, waits for them, and re-layouts: 16 us -> 0 us
  starting transfers between devices: 0.42 us -> 10.1 us
  other arithmetic: 10.4 us -> 0.98 us
  loops' own time: 5.61 us -> 0 us
    all_gather x4 -> x0, waiting for transfers between devices: 167 us -> none  [the longest x1 49.1 us: on_device(): lax.all_gather(cent_b, 'row', axis=1, tiled=True)]
    reduce_scatter x2 -> x0, waiting for transfers between devices: 156 us -> none  [the longest x1 83.8 us: on_device(): lax.psum_scatter(arrange(pull_a), ('dp', 'row'), scatter_dimension=0, til...]
    psum x1 -> x0, blocking collectives: 84.1 us -> none  [on_device(): summed = lax.psum(partial_loss, ('dp', 'row', 'col'))]
    dot_general x16 -> x0, matrix products: 60.5 us -> none  [the longest x8 35 us: tile_part(): jnp.dot(strip.astype(jnp.float32), off, preferred_element_type=jnp.float3...]
    all_to_all x0 -> x2, blocking collectives: none -> 36.7 us  [exchange(): moved = lax.all_to_all(chunks, CHIPS, 0, 0, tiled=True)]
    all_gather x2 -> x0, blocking collectives: 11.8 us -> none  [the longest x1 6.33 us: on_device(): lax.all_gather(view_a, 'dp', axis=0, tiled=True)]
    ppermute x0 -> x3, starting transfers between devices: none -> 10.1 us  [the longest x1 3.83 us: on_device(): far = lax.ppermute(near, 'dp', swap)]
    reduce_sum x9 -> x0, other arithmetic: 6.89 us -> none  [the longest x1 2.35 us: on_device(): partial_loss = 25.0 * jnp.sum(gap * gap) / (total * f_all)]
  transfers between devices with their start and end apart: 6 -> 3, of which waited for: 6 -> 3; matrix products, arithmetic and copies ran while one was open for 2% -> 0% of each run, Pallas kernels for 0% -> 0%
where the time goes in v2:
time: 55.7 us; the launch traced here: 55.5 us
  blocking collectives  36.7 us (66%)
  starting transfers between devices  10.1 us (18%)
  waiting for transfers between devices  4.34 us (8%)
  Pallas kernels  2.77 us (5%)
  other arithmetic  0.98 us (2%)
  between operations  0.65 us (1%)
    all_to_all x2, blocking collectives, exchange(): moved = lax.all_to_all(chunks, CHIPS, 0, 0, tiled=True)  36.7 us
    ppermute x1, starting transfers between devices, on_device(): far = lax.ppermute(near, 'dp', swap)  3.83 us
    ppermute x1, starting transfers between devices, on_device(): chip_sum = keep + lax.ppermute(send, 'core', swap)  3.7 us
    ppermute x1, starting transfers between devices, on_device(): theirs = lax.ppermute(mine, 'core', swap)  2.54 us
    ppermute x1, waiting for transfers between devices, on_device(): far = lax.ppermute(near, 'dp', swap)  2.28 us
    pallas_call x1, Pallas kernels, on_device(): pl.pallas_call(lambda *refs: final_kernel(n_all, f_all, *refs), out_shape...  1.69 us
  transfers between devices with their start and end apart: 3, of which 3 were waited for; matrix products, arithmetic and copies ran while one was open for 0% of the time, Pallas kernels for 0%

profile of v2, /device:TPU:1, one launch (start us, length us, event | category | flops | bytes accessed | tf_op | source)
XLA Modules:
  0.0 55.5 jit_solution(900914130156855020)
XLA Ops:
  0.6 0.9 %pad_maximum_fusion.refs_1_ = bf16[2,128,256]{2,1,0:T(8,128)(2,1)S(1)} fusion(bf16[1,128,256]{2,1,0:T(8,128)(2,1)} %bitcast.14, bf16[1,128,256]{2,1,0:T(8,128)(2,1)} %bitcast.15), kind=kLoop, calls=%fused_computation | loop fusion | flops 65536 | bytes 262144 | tf_op jit(solution)/shard_map/stack | solution.py:158
  1.5 3.8 %collective-permute-start = (bf16[2,128,256]{2,1,0:T(8,128)(2,1)S(1)}, bf16[2,128,256]{2,1,0:T(8,128)(2,1)S(1)}, u32[]{:S(2)}, u32[]{:S(2)}) collective-permute-start(bf16[2,128,256]{2,1,0:T(8,128)(2,1)S(1)} %pad_maximum_fusion.refs_1_), channel_id=1, source_target_pairs={{0,128},{128,0},{1,129},{129,1},{2,130},{130,2},{3,131},{131,3},{4... | collective-permute-start | bytes 393224 | tf_op jit(solution)/shard_map/ppermute | solution.py:159
  5.3 0.1 pad_add_fusion.refs_0_
  5.4 2.3 %collective-permute-done.refs_2_ = bf16[2,128,256]{2,1,0:T(8,128)(2,1)S(1)} collective-permute-done((bf16[2,128,256]{2,1,0:T(8,128)(2,1)S(1)}, bf16[2,128,256]{2,1,0:T(8,128)(2,1)S(1)}, u32[]{:S(2)}, u32[]{:S(2)}) %collective-permute-start) | collective-permute-done | bytes 131104 | tf_op jit(solution)/shard_map/ppermute | solution.py:159
  7.7 1.1 %gram.1 = (f32[320,128]{1,0:T(8,128)S(1)}, f32[320,128]{1,0:T(8,128)S(1)}, bf16[2,256,256]{2,1,0:T(8,128)(2,1)S(1)}, f32[2,128,256]{2,1,0:T(8,128)S(1)}) custom-call(s32[2]{0:T(128)S(1)} %pad_add_fusion.refs_0_, bf16[2,128,256]{2,1,0:T(8,128)(2,1)S(1)} %pad_maximum_fusion.refs_1_, bf16[2,128,256]{2,1,0:T(8,128)(2,1)S(1)} %collective-permute-done.refs_2_), custom_call_target="tpu_custom_call" | custom-call | tf_op jit(solution)/shard_map/gram/pallas_call | solution.py:162
  8.8 3.7 %collective-permute-start.1 = (f32[320,128]{1,0:T(8,128)S(1)}, f32[320,128]{1,0:T(8,128)S(1)}, u32[]{:S(2)}, u32[]{:S(2)}) collective-permute-start(f32[320,128]{1,0:T(8,128)S(1)} %get-tuple-element.11), channel_id=1, source_target_pairs={{0,1},{1,0},{2,3},{3,2},{4,5},{5,4},{6,7},{7,6},{8,9},{9,8},{10,11... | collective-permute-start | bytes 491528 | tf_op jit(solution)/shard_map/ppermute | solution.py:181
  12.5 1.0 %collective-permute-done.1 = f32[320,128]{1,0:T(8,128)S(1)} collective-permute-done((f32[320,128]{1,0:T(8,128)S(1)}, f32[320,128]{1,0:T(8,128)S(1)}, u32[]{:S(2)}, u32[]{:S(2)}) %collective-permute-start.1) | collective-permute-done | bytes 163872 | tf_op jit(solution)/shard_map/ppermute | solution.py:181
  13.5 21.7 %all_to_all.10 = f32[64,1,640]{2,1,0:T(1,128)S(1)} all-to-all(f32[64,1,640]{2,1,0:T(1,128)S(1)} %bitcast.13), channel_id=1, replica_groups=mesh['dp'=2,'x'=4,'yl'=2,'z'=8,'core'=2] {'x','yl','z'}, dimensions={0} | all-to-all | bytes 327680 | tf_op jit(solution)/shard_map/all_to_all | solution.py:178
  35.2 15.1 %all_to_all.11 = f32[64,1,640]{2,1,0:T(1,128)S(1)} all-to-all(f32[64,1,640]{2,1,0:T(1,128)S(1)} %bitcast.10), channel_id=1, replica_groups=mesh['dp'=2,'x'=4,'yl'=2,'z'=8,'core'=2] {'x','yl','z'}, dimensions={0} | all-to-all | bytes 327680 | tf_op jit(solution)/shard_map/all_to_all | solution.py:178
  50.3 2.5 %collective-permute-start.2 = (f32[320,128]{1,0:T(8,128)S(1)}, f32[320,128]{1,0:T(8,128)S(1)}, u32[]{:S(2)}, u32[]{:S(2)}) collective-permute-start(f32[320,128]{1,0:T(8,128)S(1)} %bitcast.11), channel_id=1, source_target_pairs={{0,1},{1,0},{2,3},{3,2},{4,5},{5,4},{6,7},{7,6},{8,9},{9,8},{10,11... | collective-permute-start | bytes 491528 | tf_op jit(solution)/shard_map/ppermute | solution.py:192
  52.8 1.0 %collective-permute-done.2.refs_2_ = f32[320,128]{1,0:T(8,128)S(1)} collective-permute-done((f32[320,128]{1,0:T(8,128)S(1)}, f32[320,128]{1,0:T(8,128)S(1)}, u32[]{:S(2)}, u32[]{:S(2)}) %collective-permute-start.2) | collective-permute-done | bytes 163872 | tf_op jit(solution)/shard_map/ppermute | solution.py:192
  53.9 1.7 %final.1 = (f32[128,256]{1,0:T(8,128)}, f32[128,256]{1,0:T(8,128)}, f32[1,1]{1,0:T(1,128)}) custom-call(s32[2]{0:T(128)S(1)} %pad_add_fusion.refs_0_, f32[320,128]{1,0:T(8,128)S(1)} %bitcast.12, f32[320,128]{1,0:T(8,128)S(1)} %collective-permute-done.2.refs_2_, bf16[2,256,256]{2,1,0:T(8,128)(2,1)S(1)} %get-tuple-element.12.refs_3_, ...), custom_call_target="tpu_custom_call" | custom-call | tf_op jit(solution)/shard_map/final/pallas_call | solution.py:193
  (2 shorter events, 0.0 us)
Async XLA Ops:
  1.5 6.2 %collective-permute-start = (bf16[2,128,256]{2,1,0:T(8,128)(2,1)S(1)}, bf16[2,128,256]{2,1,0:T(8,128)(2,1)S(1)}, u32[]{:S(2)}, u32[]{:S(2)}) collective-permute-start(bf16[2,128,256]{2,1,0:T(8,128)(2,1)S(1)} %pad_maximum_fusion.refs_1_), channel_id=1, source_target_pairs={{0,128},{128,0},{1,129},{129,1},{2,130},{130,2},{3,131},{131,3},{4... | collective-permute-start | bytes 393224 | tf_op jit(solution)/shard_map/ppermute | solution.py:159
  8.8 4.7 %collective-permute-start.1 = (f32[320,128]{1,0:T(8,128)S(1)}, f32[320,128]{1,0:T(8,128)S(1)}, u32[]{:S(2)}, u32[]{:S(2)}) collective-permute-start(f32[320,128]{1,0:T(8,128)S(1)} %get-tuple-element.11), channel_id=1, source_target_pairs={{0,1},{1,0},{2,3},{3,2},{4,5},{5,4},{6,7},{7,6},{8,9},{9,8},{10,11... | collective-permute-start | bytes 491528 | tf_op jit(solution)/shard_map/ppermute | solution.py:181
  50.3 3.6 %collective-permute-start.2 = (f32[320,128]{1,0:T(8,128)S(1)}, f32[320,128]{1,0:T(8,128)S(1)}, u32[]{:S(2)}, u32[]{:S(2)}) collective-permute-start(f32[320,128]{1,0:T(8,128)S(1)} %bitcast.11), channel_id=1, source_target_pairs={{0,1},{1,0},{2,3},{3,2},{4,5},{5,4},{6,7},{7,6},{8,9},{9,8},{10,11... | collective-permute-start | bytes 491528 | tf_op jit(solution)/shard_map/ppermute | solution.py:192

commit v3 on v2

v3 whole, which is shorter than its diff:
```python
import jax
import jax.numpy as jnp
from jax import lax
from jax.experimental import pallas as pl
from jax.experimental.pallas import tpu as pltpu
from jax.sharding import Mesh, PartitionSpec as P

AXES = ("dp", "x", "yl", "z", "core")
SPLIT = ("x", "yl", "core")
RING = ("z",)
EXTRA = 16
F32, BF16 = jnp.float32, jnp.bfloat16
ROW_DIMS = (((1,), (1,)), ((), ()))


def split3(value):
    first = value.astype(BF16)
    rest = value - first.astype(F32)
    second = rest.astype(BF16)
    third = (rest - second.astype(F32)).astype(BF16)
    return (first, second, third)


def iotas(shape):
    return (lax.broadcasted_iota(jnp.int32, shape, 0), lax.broadcasted_iota(jnp.int32, shape, 1))


def total_sum(value):
    return jnp.sum(value, axis=(0, 1), keepdims=True)


def col_sum(value):
    return jnp.sum(value, axis=0, keepdims=True)


def pack(gram):
    g00, g01, g11 = gram
    rows, cols = iotas(g00.shape)
    both = jnp.where(rows < cols, g00, g11)
    diag = col_sum(jnp.where(rows == cols, g00, F32(0.0)))
    return (both, g01, diag)


def unpack(both, diag):
    rows, cols = iotas(both.shape)
    zero = F32(0.0)
    upper = jnp.where(rows < cols, both, zero)
    lower = jnp.where(rows > cols, both, zero)
    on_diag = rows == cols
    g00 = upper + upper.T + jnp.where(on_diag, diag, zero)
    g11 = lower + lower.T + jnp.where(on_diag, both, zero)
    return (g00, g11)


def gram_kernel(n_all, f_all, place, near, far, packed, cent, base):
    n_dev = near.shape[1]
    coef = 2.0 * n_all / (25.0 * (n_all - 1))
    first_plane = place[0] == 0
    views = []
    for view in range(2):
        mine, theirs = near[view].astype(F32), far[view].astype(F32)
        views.append((jnp.where(first_plane, mine, theirs), jnp.where(first_plane, theirs, mine)))
    gap0 = views[0][0] - views[1][0]
    gap1 = views[0][1] - views[1][1]
    gap = jnp.where(first_plane, gap0, gap1)
    loss = jnp.zeros((1, 1), F32)
    diags = []
    for view, (z0, z1) in enumerate(views):
        mean = (col_sum(z0) + col_sum(z1)) / n_all
        diff0, diff1 = z0 - mean, z1 - mean
        squares = col_sum(diff0 * diff0) + col_sum(diff1 * diff1)
        std = jnp.sqrt(squares / (n_all - 1) + 0.0001)
        c0, c1 = diff0.astype(BF16), diff1.astype(BF16)
        cent[view, :n_dev] = c0
        cent[view, n_dev:] = c1
        f0, f1 = c0.astype(F32), c1.astype(F32)
        r = col_sum(f0) + col_sum(f1)
        d = (col_sum(f0 * f0) + col_sum(f1 * f1)) / (n_all - 1)
        hinge = jnp.where(std < 1.0, n_all / (2.0 * std * (n_all - 1)), F32(0.0))
        diff = jnp.where(first_plane, diff0, diff1)
        own = jnp.where(first_plane, f0, f1)
        sign = 1.0 if view == 0 else -1.0
        base[view] = sign * gap - hinge * diff - coef * (d * (own - r / n_all))
        loss = loss + (25.0 / f_all) * total_sum(jnp.maximum(1.0 - std, 0.0))
        loss = loss - total_sum(d * d) / f_all
        every = jnp.concatenate([c0, c1], axis=0)
        top = lax.dot_general(c0, every, ROW_DIMS, preferred_element_type=F32)
        low = lax.dot_general(c1, c1, ROW_DIMS, preferred_element_type=F32)
        both, g01, diag = pack((top[:, :n_dev], top[:, n_dev:], low))
        packed[view * n_all : view * n_all + n_dev] = both
        packed[view * n_all + n_dev : (view + 1) * n_all] = g01
        diags.append(diag)
    squared_gap = total_sum(gap0 * gap0) + total_sum(gap1 * gap1)
    loss = loss + (25.0 / (n_all * f_all)) * squared_gap
    rows, unused = iotas((EXTRA, n_dev))
    extra = jnp.where(rows == 2, loss, F32(0.0))
    for view, diag in enumerate(diags):
        extra = jnp.where(rows == view, diag, extra)
    packed[2 * n_all :] = extra


def share_kernel(n_in, n_out, shares, spread):
    depth = shares.shape[0] // n_in
    total = shares[:depth]
    for i in range(1, n_in):
        total = total + shares[i * depth : (i + 1) * depth]
    for i in range(n_out):
        spread[i * depth : (i + 1) * depth] = total


def final_kernel(n_all, f_all, place, packed, cent, base, grad_a, grad_b, objective):
    n_dev = base.shape[1]
    coef = 2.0 * n_all / (25.0 * (n_all - 1))
    first_plane = place[0] == 0
    square = jnp.zeros((1, 1), F32)
    extra = packed[2 * n_all :]
    for view, grad in enumerate((grad_a, grad_b)):
        both = packed[view * n_all : view * n_all + n_dev]
        g01 = packed[view * n_all + n_dev : (view + 1) * n_all]
        g00, g11 = unpack(both, extra[view : view + 1])
        g10 = g01.T
        square = square + total_sum(g00 * g00 + 2.0 * (g01 * g01) + g11 * g11)
        v0 = col_sum(g00) + col_sum(g10)
        v1 = col_sum(g01) + col_sum(g11)
        left = jnp.where(first_plane, g00, g10) - v0 / n_all
        right = jnp.where(first_plane, g01, g11) - v1 / n_all
        rows = jnp.concatenate([left, right], axis=1)
        parts = jnp.concatenate(split3(rows), axis=0)
        pulls = jnp.dot(parts, cent[view], preferred_element_type=F32)
        pull = pulls[:n_dev] + pulls[n_dev : 2 * n_dev] + pulls[2 * n_dev :]
        grad[...] = base[view] + (coef / (n_all - 1)) * pull
    loss = extra[2:3, 0:1] + square / (float(n_all - 1) * float(n_all - 1) * f_all)
    objective[...] = loss * n_all / (50.0 * f_all)


def on_device(view_a, view_b):
    n_dp = lax.axis_size("dp")
    n_split, n_ring = lax.axis_size(SPLIT), lax.axis_size(RING)
    n_dev, shard = view_a.shape
    n_all = n_dev * n_dp
    f_all = shard * n_split * n_ring
    swap = [(0, 1), (1, 0)]
    vmem = pl.BlockSpec(memory_space=pltpu.VMEM)
    smem = pl.BlockSpec(memory_space=pltpu.SMEM)
    params = pltpu.CompilerParams(vmem_limit_bytes=32 * 1024 * 1024)
    place = lax.axis_index("dp").astype(jnp.int32).reshape(1)
    near = jnp.stack([view_a, view_b])
    far = lax.ppermute(near, "dp", swap)
    n_rows = 2 * n_all + EXTRA
    depth = n_rows // n_split
    packed, cent, base = pl.pallas_call(
        lambda *refs: gram_kernel(n_all, f_all, *refs),
        out_shape=(
            jax.ShapeDtypeStruct((n_rows, n_dev), F32),
            jax.ShapeDtypeStruct((2, n_all, shard), BF16),
            jax.ShapeDtypeStruct((2, n_dev, shard), F32),
        ),
        in_specs=[smem, vmem, vmem],
        out_specs=(vmem,) * 3,
        compiler_params=params,
        name="gram",
    )(place, near, far)

    def exchange(rows, axes):
        chunks = rows.reshape(lax.axis_size(axes), 1, depth * n_dev)
        return lax.all_to_all(chunks, axes, 0, 0, tiled=True).reshape(rows.shape)

    def share(rows, n_in, n_out):
        return pl.pallas_call(
            lambda *refs: share_kernel(n_in, n_out, *refs),
            out_shape=jax.ShapeDtypeStruct((n_out * depth, n_dev), F32),
            in_specs=[vmem],
            out_specs=vmem,
            compiler_params=params,
            name="share",
        )(rows)

    pieces = share(exchange(packed, SPLIT), n_split, n_ring)
    spread = share(exchange(pieces, RING), n_ring, n_split)
    whole = exchange(spread, SPLIT)
    grad_a, grad_b, objective = pl.pallas_call(
        lambda *refs: final_kernel(n_all, f_all, *refs),
        out_shape=(
            jax.ShapeDtypeStruct((n_dev, shard), F32),
            jax.ShapeDtypeStruct((n_dev, shard), F32),
            jax.ShapeDtypeStruct((1, 1), F32),
        ),
        in_specs=[smem] + [vmem] * 3,
        out_specs=(vmem,) * 3,
        compiler_params=params,
        name="final",
    )(place, whole, cent, base)
    return (grad_a, grad_b, objective.reshape(()))


def solution(mesh):
    fine = Mesh(mesh.devices.reshape(2, 4, 2, 8, 2), AXES)
    spec = P("dp", ("x", "yl", "z", "core"))
    return jax.shard_map(
        on_device, mesh=fine, in_specs=(spec, spec), out_specs=(spec, spec, P()), check_vma=False
    )
```

time: 55.7 us -> 52.6 us (0.944)
  starting transfers between devices: 10.1 us -> 3.83 us
  blocking collectives: 36.7 us -> 42.9 us
  waiting for transfers between devices: 4.34 us -> 2.36 us
  Pallas kernels: 2.77 us -> 1.75 us
    ppermute x2 -> x0, starting transfers between devices: 6.24 us -> none  [the longest x1 3.7 us: on_device(): chip_sum = keep + lax.ppermute(send, 'core', swap)]
    all_to_all x2 -> x3, blocking collectives: 36.7 us -> 42.9 us  [exchange(): return lax.all_to_all(chunks, axes, 0, 0, tiled=True).reshape(rows.shape)]
    ppermute x2 -> x0, waiting for transfers between devices: 2.06 us -> none  [the longest x1 1.03 us: on_device(): chip_sum = keep + lax.ppermute(send, 'core', swap)]
  transfers between devices with their start and end apart: 3 -> 1, of which waited for: 3 -> 1; matrix products, arithmetic and copies ran while one was open for 0% -> 0% of each run, Pallas kernels for 0% -> 0%
where the time goes in v3:
time: 52.6 us; the launch traced here: 52.4 us
  blocking collectives  42.9 us (82%)
  starting transfers between devices  3.83 us (7%)
  waiting for transfers between devices  2.36 us (4%)
  Pallas kernels  1.75 us (3%)
  other arithmetic  0.89 us (2%)
  between operations  0.65 us (1%)
    all_to_all x3, blocking collectives, exchange(): return lax.all_to_all(chunks, axes, 0, 0, tiled=True).reshape(rows.shape)  42.9 us
    ppermute x1, starting transfers between devices, on_device(): far = lax.ppermute(near, 'dp', swap)  3.83 us
    ppermute x1, waiting for transfers between devices, on_device(): far = lax.ppermute(near, 'dp', swap)  2.36 us
    pallas_call x1, Pallas kernels, on_device(): pl.pallas_call(lambda *refs: final_kernel(n_all, f_all, *refs), out_shape...  1.14 us
  transfers between devices with their start and end apart: 1, of which 1 were waited for; matrix products, arithmetic and copies ran while one was open for 0% of the time, Pallas kernels for 0%

profile of v3, /device:TPU:1, one launch (start us, length us, event | category | flops | bytes accessed | tf_op | source)
XLA Modules:
  0.0 52.4 jit_solution(3953870591150055029)
XLA Ops:
  0.6 0.9 %pad_maximum_fusion.refs_1_ = bf16[2,128,256]{2,1,0:T(8,128)(2,1)S(1)} fusion(bf16[1,128,256]{2,1,0:T(8,128)(2,1)} %bitcast.16, bf16[1,128,256]{2,1,0:T(8,128)(2,1)} %bitcast.17), kind=kLoop, calls=%fused_computation | loop fusion | flops 65536 | bytes 262144 | tf_op jit(solution)/shard_map/stack | solution.py:147
  1.5 3.8 %collective-permute-start = (bf16[2,128,256]{2,1,0:T(8,128)(2,1)S(1)}, bf16[2,128,256]{2,1,0:T(8,128)(2,1)S(1)}, u32[]{:S(2)}, u32[]{:S(2)}) collective-permute-start(bf16[2,128,256]{2,1,0:T(8,128)(2,1)S(1)} %pad_maximum_fusion.refs_1_), channel_id=1, source_target_pairs={{0,128},{128,0},{1,129},{129,1},{2,130},{130,2},{3,131},{131,3},{4... | collective-permute-start | bytes 393224 | tf_op jit(solution)/shard_map/ppermute | solution.py:148
  5.3 2.4 %collective-permute-done.refs_2_ = bf16[2,128,256]{2,1,0:T(8,128)(2,1)S(1)} collective-permute-done((bf16[2,128,256]{2,1,0:T(8,128)(2,1)S(1)}, bf16[2,128,256]{2,1,0:T(8,128)(2,1)S(1)}, u32[]{:S(2)}, u32[]{:S(2)}) %collective-permute-start) | collective-permute-done | bytes 131104 | tf_op jit(solution)/shard_map/ppermute | solution.py:148
  7.7 0.5 %gram.1 = (f32[528,128]{1,0:T(8,128)S(1)}, bf16[2,256,256]{2,1,0:T(8,128)(2,1)S(1)}, f32[2,128,256]{2,1,0:T(8,128)S(1)}) custom-call(s32[1]{0:T(128)} %bitcast.refs_0_, bf16[2,128,256]{2,1,0:T(8,128)(2,1)S(1)} %pad_maximum_fusion.refs_1_, bf16[2,128,256]{2,1,0:T(8,128)(2,1)S(1)} %collective-permute-done.refs_2_), custom_call_target="tpu_custom_call" | custom-call | tf_op jit(solution)/shard_map/gram/pallas_call | solution.py:151
  8.3 14.7 %all_to_all.15 = f32[16,1,4224]{2,1,0:T(1,128)S(1)} all-to-all(f32[16,1,4224]{2,1,0:T(1,128)S(1)} %bitcast.15), channel_id=1, replica_groups=mesh['dp'=2,'x'=4,'yl'=2,'z'=8,'core'=2] {'x','yl','core'}, dimensions={0} | all-to-all | bytes 540672 | tf_op jit(solution)/shard_map/all_to_all | solution.py:166
  23.0 15.9 %all_to_all.16 = f32[8,1,4224]{2,1,0:T(1,128)S(1)} all-to-all(f32[8,1,4224]{2,1,0:T(1,128)S(1)} %bitcast.13), channel_id=1, replica_groups=mesh['dp'=2,'x'=4,'yl'=2,'z'=8,'core'=2] {'z'}, dimensions={0} | all-to-all | bytes 270336 | tf_op jit(solution)/shard_map/all_to_all | solution.py:166
  39.0 12.3 %all_to_all.17 = f32[16,1,4224]{2,1,0:T(1,128)S(1)} all-to-all(f32[16,1,4224]{2,1,0:T(1,128)S(1)} %bitcast.11), channel_id=1, replica_groups=mesh['dp'=2,'x'=4,'yl'=2,'z'=8,'core'=2] {'x','yl','core'}, dimensions={0} | all-to-all | bytes 540672 | tf_op jit(solution)/shard_map/all_to_all | solution.py:166
  51.3 1.1 %final.1 = (f32[128,256]{1,0:T(8,128)}, f32[128,256]{1,0:T(8,128)}, f32[1,1]{1,0:T(1,128)}) custom-call(s32[1]{0:T(128)} %bitcast.refs_0_, f32[528,128]{1,0:T(8,128)S(1)} %bitcast.12, bf16[2,256,256]{2,1,0:T(8,128)(2,1)S(1)} %get-tuple-element.10.refs_2_, f32[2,128,256]{2,1,0:T(8,128)S(1)} %get-tuple-element.11.refs_3_), custom_call_target="tpu_custom_call" | custom-call | tf_op jit(solution)/shard_map/final/pallas_call | solution.py:181
  (2 shorter events, 0.1 us)
Async XLA Ops:
  1.5 6.2 %collective-permute-start = (bf16[2,128,256]{2,1,0:T(8,128)(2,1)S(1)}, bf16[2,128,256]{2,1,0:T(8,128)(2,1)S(1)}, u32[]{:S(2)}, u32[]{:S(2)}) collective-permute-start(bf16[2,128,256]{2,1,0:T(8,128)(2,1)S(1)} %pad_maximum_fusion.refs_1_), channel_id=1, source_target_pairs={{0,128},{128,0},{1,129},{129,1},{2,130},{130,2},{3,131},{131,3},{4... | collective-permute-start | bytes 393224 | tf_op jit(solution)/shard_map/ppermute | solution.py:148

commit v4 on v3

v4 whole, which is shorter than its diff:
```python
import jax
import jax.numpy as jnp
from jax import lax
from jax.experimental import pallas as pl
from jax.experimental.pallas import tpu as pltpu
from jax.sharding import Mesh, PartitionSpec as P

N_X, N_Y, N_Z, N_CORE = 4, 2, 8, 2
RING_ORDER = (4, 0, 1, 2, 3, 5, 6, 7)
SPLIT_ORDER = ((2, 1, 1), (2, 1, 0), (3, 1, 1), (1, 1, 1), (0, 1, 1), (3, 0, 1), (2, 0, 1), (1, 0, 1), (0, 0, 1), (3, 1, 0), (1, 1, 0), (0, 1, 0), (3, 0, 0), (2, 0, 0), (1, 0, 0), (0, 0, 0))


def place_of(x, y, z, core):
    return ((x * N_Y + y) * N_Z + z) * N_CORE + core


SPLIT = [[place_of(x, y, z, c) for x, y, c in SPLIT_ORDER] for z in range(N_Z)]
RING = [[place_of(x, y, z, c) for z in RING_ORDER] for x, y, c in SPLIT_ORDER]
EXTRA = 16
F32, BF16 = jnp.float32, jnp.bfloat16
ROW_DIMS = (((1,), (1,)), ((), ()))


def split3(value):
    first = value.astype(BF16)
    rest = value - first.astype(F32)
    second = rest.astype(BF16)
    third = (rest - second.astype(F32)).astype(BF16)
    return (first, second, third)


def iotas(shape):
    return (lax.broadcasted_iota(jnp.int32, shape, 0), lax.broadcasted_iota(jnp.int32, shape, 1))


def total_sum(value):
    return jnp.sum(value, axis=(0, 1), keepdims=True)


def col_sum(value):
    return jnp.sum(value, axis=0, keepdims=True)


def pack(gram):
    g00, g01, g11 = gram
    rows, cols = iotas(g00.shape)
    both = jnp.where(rows < cols, g00, g11)
    diag = col_sum(jnp.where(rows == cols, g00, F32(0.0)))
    return (both, g01, diag)


def gram_kernel(n_all, f_all, place, near, far, packed, cent, base):
    @pl.when(place[0] == 0)
    def _():
        gram_body(n_all, f_all, (near, far), 0, packed, cent, base)

    @pl.when(place[0] != 0)
    def _():
        gram_body(n_all, f_all, (far, near), 1, packed, cent, base)


def gram_body(n_all, f_all, halves, plane, packed, cent, base):
    n_dev = halves[0].shape[1]
    coef = 2.0 * n_all / (25.0 * (n_all - 1))
    views = [[half[view].astype(F32) for half in halves] for view in range(2)]
    gaps = [views[0][i] - views[1][i] for i in range(2)]
    loss = jnp.zeros((1, 1), F32)
    diags = []
    for view, zs in enumerate(views):
        mean = (col_sum(zs[0]) + col_sum(zs[1])) / n_all
        diffs = [z - mean for z in zs]
        squares = col_sum(diffs[0] * diffs[0] + diffs[1] * diffs[1])
        std = jnp.sqrt(squares / (n_all - 1) + 0.0001)
        cs = [diff.astype(BF16) for diff in diffs]
        cent[view, :n_dev] = cs[0]
        cent[view, n_dev:] = cs[1]
        every = jnp.concatenate(cs, axis=0)
        top = lax.dot_general(cs[0], every, ROW_DIMS, preferred_element_type=F32)
        low = lax.dot_general(cs[1], cs[1], ROW_DIMS, preferred_element_type=F32)
        fs = [c.astype(F32) for c in cs]
        r = col_sum(fs[0] + fs[1])
        d = col_sum(fs[0] * fs[0] + fs[1] * fs[1]) / (n_all - 1)
        hinge = jnp.where(std < 1.0, n_all / (2.0 * std * (n_all - 1)), F32(0.0))
        pulled = coef * d
        rest = gaps[plane] if view == 0 else -gaps[plane]
        base[view] = rest - hinge * diffs[plane] - pulled * fs[plane] + pulled * (r / n_all)
        terms = 25.0 * jnp.maximum(1.0 - std, 0.0) - d * d
        loss = loss + total_sum(terms) / f_all
        both, g01, diag = pack((top[:, :n_dev], top[:, n_dev:], low))
        packed[view * n_all : view * n_all + n_dev] = both
        packed[view * n_all + n_dev : (view + 1) * n_all] = g01
        diags.append(diag)
    squared_gap = total_sum(gaps[0] * gaps[0] + gaps[1] * gaps[1])
    loss = loss + (25.0 / (n_all * f_all)) * squared_gap
    rows, unused = iotas((EXTRA, n_dev))
    extra = jnp.where(rows == 2, loss, F32(0.0))
    for view, diag in enumerate(diags):
        extra = jnp.where(rows == view, diag, extra)
    packed[2 * n_all :] = extra


def share_kernel(n_in, n_out, shares, spread):
    depth = shares.shape[0] // n_in
    total = shares[:depth]
    for i in range(1, n_in):
        total = total + shares[i * depth : (i + 1) * depth]
    for i in range(n_out):
        spread[i * depth : (i + 1) * depth] = total


def final_kernel(n_all, f_all, place, packed, cent, base, grad_a, grad_b, objective):
    n_dev = base.shape[1]
    coef = 2.0 * n_all / (25.0 * (n_all - 1))
    first_plane = place[0] == 0
    rows, cols = iotas((n_dev, n_dev))
    on_diag, above = rows == cols, rows < cols
    zero = F32(0.0)
    square = jnp.zeros((1, 1), F32)
    extra = packed[2 * n_all :]
    for view, grad in enumerate((grad_a, grad_b)):
        both = packed[view * n_all : view * n_all + n_dev]
        g01 = packed[view * n_all + n_dev : (view + 1) * n_all]
        diag0 = extra[view : view + 1]
        diag1 = col_sum(jnp.where(on_diag, both, zero))
        square = square + 2.0 * total_sum(both * both + g01 * g01)
        square = square + total_sum(diag0 * diag0 - diag1 * diag1)
        turned, g10 = both.T, g01.T
        g00 = jnp.where(above, both, jnp.where(on_diag, diag0, turned))
        g11 = jnp.where(above, turned, both)
        v0 = col_sum(g00 + g10) / n_all
        v1 = col_sum(g01 + g11) / n_all
        left = jnp.where(first_plane, g00, g10) - v0
        right = jnp.where(first_plane, g01, g11) - v1
        parts = jnp.concatenate(split3(jnp.concatenate([left, right], axis=1)), axis=0)
        pulls = jnp.dot(parts, cent[view], preferred_element_type=F32)
        pull = pulls[:n_dev] + pulls[n_dev : 2 * n_dev] + pulls[2 * n_dev :]
        grad[...] = base[view] + (coef / (n_all - 1)) * pull
    loss = extra[2:3, 0:1] + square / (float(n_all - 1) * float(n_all - 1) * f_all)
    objective[...] = loss * n_all / (50.0 * f_all)


def on_device(view_a, view_b):
    n_dp = lax.axis_size("dp")
    n_split, n_ring = len(SPLIT_ORDER), len(RING_ORDER)
    n_dev, shard = view_a.shape
    n_all = n_dev * n_dp
    f_all = shard * n_split * n_ring
    swap = [(0, 1), (1, 0)]
    vmem = pl.BlockSpec(memory_space=pltpu.VMEM)
    smem = pl.BlockSpec(memory_space=pltpu.SMEM)
    params = pltpu.CompilerParams(vmem_limit_bytes=32 * 1024 * 1024)
    place = lax.axis_index("dp").astype(jnp.int32).reshape(1)
    near = jnp.stack([view_a, view_b])
    far = lax.ppermute(near, "dp", swap)
    n_rows = 2 * n_all + EXTRA
    depth = n_rows // n_split
    packed, cent, base = pl.pallas_call(
        lambda *refs: gram_kernel(n_all, f_all, *refs),
        out_shape=(
            jax.ShapeDtypeStruct((n_rows, n_dev), F32),
            jax.ShapeDtypeStruct((2, n_all, shard), BF16),
            jax.ShapeDtypeStruct((2, n_dev, shard), F32),
        ),
        in_specs=[smem, vmem, vmem],
        out_specs=(vmem,) * 3,
        compiler_params=params,
        name="gram",
    )(place, near, far)

    def exchange(rows, groups):
        chunks = rows.reshape(len(groups[0]), 1, depth * n_dev)
        moved = lax.all_to_all(chunks, "f", 0, 0, axis_index_groups=groups, tiled=True)
        return moved.reshape(rows.shape)

    def share(rows, n_in, n_out):
        return pl.pallas_call(
            lambda *refs: share_kernel(n_in, n_out, *refs),
            out_shape=jax.ShapeDtypeStruct((n_out * depth, n_dev), F32),
            in_specs=[vmem],
            out_specs=vmem,
            compiler_params=params,
            name="share",
        )(rows)

    pieces = share(exchange(packed, SPLIT), n_split, n_ring)
    spread = share(exchange(pieces, RING), n_ring, n_split)
    whole = exchange(spread, SPLIT)
    grad_a, grad_b, objective = pl.pallas_call(
        lambda *refs: final_kernel(n_all, f_all, *refs),
        out_shape=(
            jax.ShapeDtypeStruct((n_dev, shard), F32),
            jax.ShapeDtypeStruct((n_dev, shard), F32),
            jax.ShapeDtypeStruct((1, 1), F32),
        ),
        in_specs=[smem] + [vmem] * 3,
        out_specs=(vmem,) * 3,
        compiler_params=params,
        name="final",
    )(place, whole, cent, base)
    return (grad_a, grad_b, objective.reshape(()))


def solution(mesh):
    n_dp, n_row, n_col = (mesh.shape[name] for name in ("dp", "row", "col"))
    flat = Mesh(mesh.devices.reshape(n_dp, n_row * n_col), ("dp", "f"))
    spec = P("dp", "f")
    return jax.shard_map(
        on_device, mesh=flat, in_specs=(spec, spec), out_specs=(spec, spec, P()), check_vma=False
    )
```

time: 52.6 us -> 45.7 us (0.87)
  blocking collectives: 42.9 us -> 36.2 us
    all_to_all x3, blocking collectives: 42.9 us -> 36.2 us  [exchange(): lax.all_to_all(chunks, 'f', 0, 0, axis_index_groups=groups, tiled=True)]
where the time goes in v4:
time: 45.7 us; the launch traced here: 45.5 us
  blocking collectives  36.2 us (79%)
  starting transfers between devices  3.83 us (8%)
  waiting for transfers between devices  2.36 us (5%)
  Pallas kernels  1.62 us (4%)
  other arithmetic  0.89 us (2%)
  between operations  0.66 us (1%)
    all_to_all x3, blocking collectives, exchange(): lax.all_to_all(chunks, 'f', 0, 0, axis_index_groups=groups, tiled=True)  36.2 us
    ppermute x1, starting transfers between devices, on_device(): far = lax.ppermute(near, 'dp', swap)  3.83 us
    ppermute x1, waiting for transfers between devices, on_device(): far = lax.ppermute(near, 'dp', swap)  2.36 us
    pallas_call x1, Pallas kernels, on_device(): pl.pallas_call(lambda *refs: final_kernel(n_all, f_all, *refs), out_shape...  1.1 us
  transfers between devices with their start and end apart: 1, of which 1 were waited for; matrix products, arithmetic and copies ran while one was open for 0% of the time, Pallas kernels for 0%

profile of v4, /device:TPU:1, one launch (start us, length us, event | category | flops | bytes accessed | tf_op | source)
XLA Modules:
  0.0 45.5 jit_solution(1235474924888353778)
XLA Ops:
  0.6 0.9 %pad_maximum_fusion.refs_1_ = bf16[2,128,256]{2,1,0:T(8,128)(2,1)S(1)} fusion(bf16[1,128,256]{2,1,0:T(8,128)(2,1)} %bitcast.16, bf16[1,128,256]{2,1,0:T(8,128)(2,1)} %bitcast.17), kind=kLoop, calls=%fused_computation | loop fusion | flops 65536 | bytes 262144 | tf_op jit(solution)/shard_map/stack | solution.py:153
  1.5 3.8 %collective-permute-start = (bf16[2,128,256]{2,1,0:T(8,128)(2,1)S(1)}, bf16[2,128,256]{2,1,0:T(8,128)(2,1)S(1)}, u32[]{:S(2)}, u32[]{:S(2)}) collective-permute-start(bf16[2,128,256]{2,1,0:T(8,128)(2,1)S(1)} %pad_maximum_fusion.refs_1_), channel_id=1, source_target_pairs={{0,128},{128,0},{1,129},{129,1},{2,130},{130,2},{3,131},{131,3},{4... | collective-permute-start | bytes 393224 | tf_op jit(solution)/shard_map/ppermute | solution.py:154
  5.3 2.4 %collective-permute-done.refs_2_ = bf16[2,128,256]{2,1,0:T(8,128)(2,1)S(1)} collective-permute-done((bf16[2,128,256]{2,1,0:T(8,128)(2,1)S(1)}, bf16[2,128,256]{2,1,0:T(8,128)(2,1)S(1)}, u32[]{:S(2)}, u32[]{:S(2)}) %collective-permute-start) | collective-permute-done | bytes 131104 | tf_op jit(solution)/shard_map/ppermute | solution.py:154
  7.7 0.5 gram.1
  8.2 12.8 %all_to_all.15 = f32[16,1,4224]{2,1,0:T(1,128)S(1)} all-to-all(f32[16,1,4224]{2,1,0:T(1,128)S(1)} %bitcast.15), channel_id=1, replica_groups={{81,80,113,49,17,97,65,33,1,112,48,16,96,64,32,0},{83,82,115,51,19,99,6..., dimensions={0} | all-to-all | bytes 540672 | tf_op jit(solution)/shard_map/all_to_all | solution.py:172
  21.0 11.7 %all_to_all.16 = f32[8,1,4224]{2,1,0:T(1,128)S(1)} all-to-all(f32[8,1,4224]{2,1,0:T(1,128)S(1)} %bitcast.13), channel_id=1, replica_groups={{89,81,83,85,87,91,93,95},{88,80,82,84,86,90,92,94},{121,113,115,117,11..., dimensions={0} | all-to-all | bytes 270336 | tf_op jit(solution)/shard_map/all_to_all | solution.py:172
  32.8 11.6 %all_to_all.17 = f32[16,1,4224]{2,1,0:T(1,128)S(1)} all-to-all(f32[16,1,4224]{2,1,0:T(1,128)S(1)} %bitcast.11), channel_id=1, replica_groups={{81,80,113,49,17,97,65,33,1,112,48,16,96,64,32,0},{83,82,115,51,19,99,6..., dimensions={0} | all-to-all | bytes 540672 | tf_op jit(solution)/shard_map/all_to_all | solution.py:172
  44.4 1.1 %final.1 = (f32[128,256]{1,0:T(8,128)}, f32[128,256]{1,0:T(8,128)}, f32[1,1]{1,0:T(1,128)}) custom-call(s32[1]{0:T(128)} %bitcast.refs_0_, f32[528,128]{1,0:T(8,128)S(1)} %bitcast.12, bf16[2,256,256]{2,1,0:T(8,128)(2,1)S(1)} %get-tuple-element.10.refs_2_, f32[2,128,256]{2,1,0:T(8,128)S(1)} %get-tuple-element.11.refs_3_), custom_call_target="tpu_custom_call" | custom-call | tf_op jit(solution)/shard_map/final/pallas_call | solution.py:188
  (2 shorter events, 0.1 us)
Async XLA Ops:
  1.5 6.2 %collective-permute-start = (bf16[2,128,256]{2,1,0:T(8,128)(2,1)S(1)}, bf16[2,128,256]{2,1,0:T(8,128)(2,1)S(1)}, u32[]{:S(2)}, u32[]{:S(2)}) collective-permute-start(bf16[2,128,256]{2,1,0:T(8,128)(2,1)S(1)} %pad_maximum_fusion.refs_1_), channel_id=1, source_target_pairs={{0,128},{128,0},{1,129},{129,1},{2,130},{130,2},{3,131},{131,3},{4... | collective-permute-start | bytes 393224 | tf_op jit(solution)/shard_map/ppermute | solution.py:154

commit v5 on v4

--- a/solution.py
+++ b/solution.py
@@ -6,8 +6,8 @@
 from jax.sharding import Mesh, PartitionSpec as P
 
 N_X, N_Y, N_Z, N_CORE = 4, 2, 8, 2
-RING_ORDER = (4, 0, 1, 2, 3, 5, 6, 7)
-SPLIT_ORDER = ((2, 1, 1), (2, 1, 0), (3, 1, 1), (1, 1, 1), (0, 1, 1), (3, 0, 1), (2, 0, 1), (1, 0, 1), (0, 0, 1), (3, 1, 0), (1, 1, 0), (0, 1, 0), (3, 0, 0), (2, 0, 0), (1, 0, 0), (0, 0, 0))
+RING_ORDER = (5, 6, 3, 2, 1, 0, 4, 7)
+SPLIT_ORDER = ((2, 1, 1), (0, 1, 0), (1, 1, 0), (3, 1, 0), (2, 0, 0), (2, 1, 0), (1, 0, 0), (3, 0, 0), (0, 0, 0), (1, 1, 1), (3, 1, 1), (1, 0, 1), (0, 1, 1), (2, 0, 1), (3, 0, 1), (0, 0, 1))
 
 
 def place_of(x, y, z, core):
@@ -16,7 +16,11 @@
 
 SPLIT = [[place_of(x, y, z, c) for x, y, c in SPLIT_ORDER] for z in range(N_Z)]
 RING = [[place_of(x, y, z, c) for z in RING_ORDER] for x, y, c in SPLIT_ORDER]
-EXTRA = 16
+FOLD, CROSS = 4, 8
+PER_VIEW = 2 * FOLD + CROSS
+DEPTH = 2 * PER_VIEW + 1
+OUT_VIEW = FOLD + CROSS
+OUT_DEPTH = 2 * OUT_VIEW + 2
 F32, BF16 = jnp.float32, jnp.bfloat16
 ROW_DIMS = (((1,), (1,)), ((), ()))
 
@@ -41,12 +45,37 @@
     return jnp.sum(value, axis=0, keepdims=True)
 
 
-def pack(gram):
-    g00, g01, g11 = gram
-    rows, cols = iotas(g00.shape)
-    both = jnp.where(rows < cols, g00, g11)
-    diag = col_sum(jnp.where(rows == cols, g00, F32(0.0)))
-    return (both, g01, diag)
+def roll_half(value):
+    return pltpu.roll(value, value.shape[1] // 2, 1)
+
+
+def fold(gram):
+    half = gram.shape[0] // 2
+    top, low = gram[:half], roll_half(gram[half:])
+    rows, cols = iotas(top.shape)
+    return jnp.where(rows < cols, top, low)
+
+
+def unfold(folded, diag):
+    square = jnp.concatenate([folded, roll_half(folded)], axis=0)
+    turned = square.T
+    rows, cols = iotas(square.shape)
+    half = square.shape[0] // 2
+    first = jnp.where(rows < cols, square, jnp.where(rows == cols, diag, turned))
+    second = jnp.where(rows < cols, turned, square)
+    return jnp.where((rows >= half) & (cols >= half), second, first)
+
+
+def put_rows(ref, depth, start, value):
+    chunks = ref.shape[0] // depth
+    for j in range(value.shape[0] // chunks):
+        ref[pl.ds(start + j, chunks, stride=depth), :] = value[j * chunks : (j + 1) * chunks]
+
+
+def take_rows(ref, depth, start, count):
+    chunks = ref.shape[0] // depth
+    parts = [ref[pl.ds(start + j, chunks, stride=depth), :] for j in range(count)]
+    return jnp.concatenate(parts, axis=0)
 
 
 def gram_kernel(n_all, f_all, place, near, far, packed, cent, base):
@@ -65,7 +94,7 @@
     views = [[half[view].astype(F32) for half in halves] for view in range(2)]
     gaps = [views[0][i] - views[1][i] for i in range(2)]
     loss = jnp.zeros((1, 1), F32)
-    diags = []
+    lines = []
     for view, zs in enumerate(views):
         mean = (col_sum(zs[0]) + col_sum(zs[1])) / n_all
         diffs = [z - mean for z in zs]
@@ -86,56 +115,78 @@
         base[view] = rest - hinge * diffs[plane] - pulled * fs[plane] + pulled * (r / n_all)
         terms = 25.0 * jnp.maximum(1.0 - std, 0.0) - d * d
         loss = loss + total_sum(terms) / f_all
-        both, g01, diag = pack((top[:, :n_dev], top[:, n_dev:], low))
-        packed[view * n_all : view * n_all + n_dev] = both
-        packed[view * n_all + n_dev : (view + 1) * n_all] = g01
-        diags.append(diag)
+        g00, g01 = top[:, :n_dev], top[:, n_dev:]
+        put_rows(packed, DEPTH, view * PER_VIEW, fold(g00))
+        put_rows(packed, DEPTH, view * PER_VIEW + FOLD, fold(low))
+        put_rows(packed, DEPTH, view * PER_VIEW + 2 * FOLD, g01)
+        rows, cols = iotas(g00.shape)
+        for block in (g00, low):
+            lines.append(col_sum(jnp.where(rows == cols, block, F32(0.0))))
+            lines.append(col_sum(block))
     squared_gap = total_sum(gaps[0] * gaps[0] + gaps[1] * gaps[1])
     loss = loss + (25.0 / (n_all * f_all)) * squared_gap
-    rows, unused = iotas((EXTRA, n_dev))
-    extra = jnp.where(rows == 2, loss, F32(0.0))
-    for view, diag in enumerate(diags):
-        extra = jnp.where(rows == view, diag, extra)
-    packed[2 * n_all :] = extra
-
-
-def share_kernel(n_in, n_out, shares, spread):
-    depth = shares.shape[0] // n_in
-    total = shares[:depth]
-    for i in range(1, n_in):
-        total = total + shares[i * depth : (i + 1) * depth]
-    for i in range(n_out):
-        spread[i * depth : (i + 1) * depth] = total
+    rows, unused = iotas((packed.shape[0] // DEPTH, n_dev))
+    extra = jnp.where(rows == len(lines), loss, F32(0.0))
+    for i, line in enumerate(lines):
+        extra = jnp.where(rows == i, line, extra)
+    put_rows(packed, DEPTH, DEPTH - 1, extra)
+
+
+def chunk_sum(shares):
+    total = shares[:DEPTH]
+    for i in range(1, shares.shape[0] // DEPTH):
+        total = total + shares[i * DEPTH : (i + 1) * DEPTH]
+    return total
+
+
+def share_kernel(shares, spread):
+    total = chunk_sum(shares)
+    for i in range(spread.shape[0] // DEPTH):
+        spread[i * DEPTH : (i + 1) * DEPTH] = total
+
+
+def spread_kernel(place, shares, spread):
+    total = chunk_sum(shares)
+    first_plane = place[0] == 0
+    pieces = []
+    for view in range(2):
+        start = view * PER_VIEW
+        block0, block1 = total[start : start + FOLD], total[start + FOLD : start + 2 * FOLD]
+        pieces.append(jnp.where(first_plane, block0, block1))
+        pieces.append(total[start + 2 * FOLD : start + PER_VIEW])
+    pieces.append(total[DEPTH - 1 :])
+    body = total[: DEPTH - 1]
+    pieces.append(jnp.broadcast_to(2.0 * total_sum(body * body), (1, total.shape[1])))
+    chunk = jnp.concatenate(pieces, axis=0)
+    for i in range(spread.shape[0] // OUT_DEPTH):
+        spread[i * OUT_DEPTH : (i + 1) * OUT_DEPTH] = chunk
 
 
 def final_kernel(n_all, f_all, place, packed, cent, base, grad_a, grad_b, objective):
     n_dev = base.shape[1]
     coef = 2.0 * n_all / (25.0 * (n_all - 1))
     first_plane = place[0] == 0
-    rows, cols = iotas((n_dev, n_dev))
-    on_diag, above = rows == cols, rows < cols
-    zero = F32(0.0)
-    square = jnp.zeros((1, 1), F32)
-    extra = packed[2 * n_all :]
+    extra = take_rows(packed, OUT_DEPTH, OUT_DEPTH - 2, 1)
+    norms = take_rows(packed, OUT_DEPTH, OUT_DEPTH - 1, 1)
+    square = jnp.sum(norms[:, 0:1], axis=0, keepdims=True)
+    unused, lanes = iotas((1, n_dev))
     for view, grad in enumerate((grad_a, grad_b)):
-        both = packed[view * n_all : view * n_all + n_dev]
-        g01 = packed[view * n_all + n_dev : (view + 1) * n_all]
-        diag0 = extra[view : view + 1]
-        diag1 = col_sum(jnp.where(on_diag, both, zero))
-        square = square + 2.0 * total_sum(both * both + g01 * g01)
-        square = square + total_sum(diag0 * diag0 - diag1 * diag1)
-        turned, g10 = both.T, g01.T
-        g00 = jnp.where(above, both, jnp.where(on_diag, diag0, turned))
-        g11 = jnp.where(above, turned, both)
-        v0 = col_sum(g00 + g10) / n_all
-        v1 = col_sum(g01 + g11) / n_all
-        left = jnp.where(first_plane, g00, g10) - v0
-        right = jnp.where(first_plane, g01, g11) - v1
+        folded = take_rows(packed, OUT_DEPTH, view * OUT_VIEW, FOLD)
+        g01 = take_rows(packed, OUT_DEPTH, view * OUT_VIEW + FOLD, CROSS)
+        diag0, sum0, diag1, sum1 = (extra[4 * view + i : 4 * view + i + 1] for i in range(4))
+        diags = diag0 * diag0 + diag1 * diag1
+        square = square + total_sum(jnp.where(lanes < n_dev // 2, diags, -diags))
+        block = unfold(folded, jnp.where(first_plane, diag0, diag1))
+        g10 = g01.T
+        v0 = (sum0 + col_sum(g10)) / n_all
+        v1 = (sum1 + col_sum(g01)) / n_all
+        left = jnp.where(first_plane, block, g10) - v0
+        right = jnp.where(first_plane, g01, block) - v1
         parts = jnp.concatenate(split3(jnp.concatenate([left, right], axis=1)), axis=0)
         pulls = jnp.dot(parts, cent[view], preferred_element_type=F32)
         pull = pulls[:n_dev] + pulls[n_dev : 2 * n_dev] + pulls[2 * n_dev :]
         grad[...] = base[view] + (coef / (n_all - 1)) * pull
-    loss = extra[2:3, 0:1] + square / (float(n_all - 1) * float(n_all - 1) * f_all)
+    loss = extra[8:9, 0:1] + square / (float(n_all - 1) * float(n_all - 1) * f_all)
     objective[...] = loss * n_all / (50.0 * f_all)
 
 
@@ -152,8 +203,7 @@
     place = lax.axis_index("dp").astype(jnp.int32).reshape(1)
     near = jnp.stack([view_a, view_b])
     far = lax.ppermute(near, "dp", swap)
-    n_rows = 2 * n_all + EXTRA
-    depth = n_rows // n_split
+    n_rows = n_split * DEPTH
     packed, cent, base = pl.pallas_call(
         lambda *refs: gram_kernel(n_all, f_all, *refs),
         out_shape=(
@@ -168,22 +218,28 @@
     )(place, near, far)
 
     def exchange(rows, groups):
-        chunks = rows.reshape(len(groups[0]), 1, depth * n_dev)
+        count = len(groups[0])
+        chunks = rows.reshape(count, 1, rows.shape[0] // count * n_dev)
         moved = lax.all_to_all(chunks, "f", 0, 0, axis_index_groups=groups, tiled=True)
         return moved.reshape(rows.shape)
 
-    def share(rows, n_in, n_out):
-        return pl.pallas_call(
-            lambda *refs: share_kernel(n_in, n_out, *refs),
-            out_shape=jax.ShapeDtypeStruct((n_out * depth, n_dev), F32),
-            in_specs=[vmem],
-            out_specs=vmem,
-            compiler_params=params,
-            name="share",
-        )(rows)
-
-    pieces = share(exchange(packed, SPLIT), n_split, n_ring)
-    spread = share(exchange(pieces, RING), n_ring, n_split)
+    shares = exchange(packed, SPLIT)
+    pieces = pl.pallas_call(
+        share_kernel,
+        out_shape=jax.ShapeDtypeStruct((n_ring * DEPTH, n_dev), F32),
+        in_specs=[vmem],
+        out_specs=vmem,
+        compiler_params=params,
+        name="share",
+    )(shares)
+    spread = pl.pallas_call(
+        spread_kernel,
+        out_shape=jax.ShapeDtypeStruct((n_split * OUT_DEPTH, n_dev), F32),
+        in_specs=[smem, vmem],
+        out_specs=vmem,
+        compiler_params=params,
+        name="spread",
+    )(place, exchange(pieces, RING))
     whole = exchange(spread, SPLIT)
     grad_a, grad_b, objective = pl.pallas_call(
         lambda *refs: final_kernel(n_all, f_all, *refs),

time: 45.7 us -> 45 us (0.985)
  blocking collectives: 36.2 us -> 35.4 us
    all_to_all x3, blocking collectives: 36.2 us -> 35.4 us  [exchange(): lax.all_to_all(chunks, 'f', 0, 0, axis_index_groups=groups, tiled=True)]
where the time goes in v5:
time: 45 us; the launch traced here: 44.8 us
  blocking collectives  35.4 us (79%)
  starting transfers between devices  3.83 us (9%)
  waiting for transfers between devices  2.36 us (5%)
  Pallas kernels  1.72 us (4%)
  other arithmetic  0.89 us (2%)
  between operations  0.65 us (1%)
    all_to_all x3, blocking collectives, exchange(): lax.all_to_all(chunks, 'f', 0, 0, axis_index_groups=groups, tiled=True)  35.4 us
    ppermute x1, starting transfers between devices, on_device(): far = lax.ppermute(near, 'dp', swap)  3.83 us
    ppermute x1, waiting for transfers between devices, on_device(): far = lax.ppermute(near, 'dp', swap)  2.36 us
    pallas_call x1, Pallas kernels, on_device(): pl.pallas_call(lambda *refs: final_kernel(n_all, f_all, *refs), out_shape...  1.09 us
  transfers between devices with their start and end apart: 1, of which 1 were waited for; matrix products, arithmetic and copies ran while one was open for 0% of the time, Pallas kernels for 0%

profile of v5, /device:TPU:1, one launch (start us, length us, event | category | flops | bytes accessed | tf_op | source)
XLA Modules:
  0.0 44.8 jit_solution(4421693658773389115)
XLA Ops:
  0.6 0.9 %pad_maximum_fusion.refs_1_ = bf16[2,128,256]{2,1,0:T(8,128)(2,1)S(1)} fusion(bf16[1,128,256]{2,1,0:T(8,128)(2,1)} %bitcast.16, bf16[1,128,256]{2,1,0:T(8,128)(2,1)} %bitcast.17), kind=kLoop, calls=%fused_computation | loop fusion | flops 65536 | bytes 262144 | tf_op jit(solution)/shard_map/stack | solution.py:204
  1.5 3.8 %collective-permute-start = (bf16[2,128,256]{2,1,0:T(8,128)(2,1)S(1)}, bf16[2,128,256]{2,1,0:T(8,128)(2,1)S(1)}, u32[]{:S(2)}, u32[]{:S(2)}) collective-permute-start(bf16[2,128,256]{2,1,0:T(8,128)(2,1)S(1)} %pad_maximum_fusion.refs_1_), channel_id=1, source_target_pairs={{0,128},{128,0},{1,129},{129,1},{2,130},{130,2},{3,131},{131,3},{4... | collective-permute-start | bytes 393224 | tf_op jit(solution)/shard_map/ppermute | solution.py:205
  5.3 2.4 %collective-permute-done.refs_2_ = bf16[2,128,256]{2,1,0:T(8,128)(2,1)S(1)} collective-permute-done((bf16[2,128,256]{2,1,0:T(8,128)(2,1)S(1)}, bf16[2,128,256]{2,1,0:T(8,128)(2,1)S(1)}, u32[]{:S(2)}, u32[]{:S(2)}) %collective-permute-start) | collective-permute-done | bytes 131104 | tf_op jit(solution)/shard_map/ppermute | solution.py:205
  7.7 0.5 %gram.1 = (f32[528,128]{1,0:T(8,128)S(1)}, bf16[2,256,256]{2,1,0:T(8,128)(2,1)S(1)}, f32[2,128,256]{2,1,0:T(8,128)S(1)}) custom-call(s32[1]{0:T(128)} %bitcast.refs_0_.place, bf16[2,128,256]{2,1,0:T(8,128)(2,1)S(1)} %pad_maximum_fusion.refs_1_, bf16[2,128,256]{2,1,0:T(8,128)(2,1)S(1)} %collective-permute-done.refs_2_), custom_call_target="tpu_custom_call" | custom-call | tf_op jit(solution)/shard_map/gram/pallas_call | solution.py:207
  8.2 12.7 %all_to_all.15 = f32[16,1,4224]{2,1,0:T(1,128)S(1)} all-to-all(f32[16,1,4224]{2,1,0:T(1,128)S(1)} %bitcast.15), channel_id=1, replica_groups={{81,16,48,112,64,80,32,96,0,49,113,33,17,65,97,1},{83,18,50,114,66,82,3..., dimensions={0} | all-to-all | bytes 540672 | tf_op jit(solution)/shard_map/all_to_all | solution.py:223
  21.0 11.7 %all_to_all.16 = f32[8,1,4224]{2,1,0:T(1,128)S(1)} all-to-all(f32[8,1,4224]{2,1,0:T(1,128)S(1)} %bitcast.13), channel_id=1, replica_groups={{91,93,87,85,83,81,89,95},{26,28,22,20,18,16,24,30},{58,60,54,52,50,48,..., dimensions={0} | all-to-all | bytes 270336 | tf_op jit(solution)/shard_map/all_to_all | solution.py:223
  32.7 0.1 spread.1
  32.8 10.9 %all_to_all.17 = f32[16,1,3328]{2,1,0:T(1,128)S(1)} all-to-all(f32[16,1,3328]{2,1,0:T(1,128)S(1)} %bitcast.12), channel_id=1, replica_groups={{81,16,48,112,64,80,32,96,0,49,113,33,17,65,97,1},{83,18,50,114,66,82,3..., dimensions={0} | all-to-all | bytes 425984 | tf_op jit(solution)/shard_map/all_to_all | solution.py:223
  43.7 1.1 %final.1 = (f32[128,256]{1,0:T(8,128)}, f32[128,256]{1,0:T(8,128)}, f32[1,1]{1,0:T(1,128)}) custom-call(s32[1]{0:T(128)} %bitcast.refs_0_.place, f32[416,128]{1,0:T(8,128)S(1)} %bitcast.11, bf16[2,256,256]{2,1,0:T(8,128)(2,1)S(1)} %get-tuple-element.10.refs_2_, f32[2,128,256]{2,1,0:T(8,128)S(1)} %get-tuple-element.11.refs_3_), custom_call_target="tpu_custom_call" | custom-call | tf_op jit(solution)/shard_map/final/pallas_call | solution.py:244
  (1 shorter events, 0.0 us)
Async XLA Ops:
  1.5 6.2 %collective-permute-start = (bf16[2,128,256]{2,1,0:T(8,128)(2,1)S(1)}, bf16[2,128,256]{2,1,0:T(8,128)(2,1)S(1)}, u32[]{:S(2)}, u32[]{:S(2)}) collective-permute-start(bf16[2,128,256]{2,1,0:T(8,128)(2,1)S(1)} %pad_maximum_fusion.refs_1_), channel_id=1, source_target_pairs={{0,128},{128,0},{1,129},{129,1},{2,130},{130,2},{3,131},{131,3},{4... | collective-permute-start | bytes 393224 | tf_op jit(solution)/shard_map/ppermute | solution.py:205

commit v6 on v5

--- a/solution.py
+++ b/solution.py
@@ -7,7 +7,7 @@
 
 N_X, N_Y, N_Z, N_CORE = 4, 2, 8, 2
 RING_ORDER = (5, 6, 3, 2, 1, 0, 4, 7)
-SPLIT_ORDER = ((2, 1, 1), (0, 1, 0), (1, 1, 0), (3, 1, 0), (2, 0, 0), (2, 1, 0), (1, 0, 0), (3, 0, 0), (0, 0, 0), (1, 1, 1), (3, 1, 1), (1, 0, 1), (0, 1, 1), (2, 0, 1), (3, 0, 1), (0, 0, 1))
+SPLIT_ORDER = ((2, 1, 1), (3, 1, 1), (2, 1, 0), (2, 0, 1), (1, 1, 1), (2, 0, 0), (3, 1, 0), (1, 1, 0), (0, 0, 1), (3, 0, 1), (3, 0, 0), (1, 0, 1), (1, 0, 0), (0, 0, 0), (0, 1, 1), (0, 1, 0))
 
 
 def place_of(x, y, z, core):

time: 45 us -> 44.6 us (level)
  blocking collectives: 35.4 us -> 34.9 us
    all_to_all x3, blocking collectives: 35.4 us -> 34.9 us  [exchange(): lax.all_to_all(chunks, 'f', 0, 0, axis_index_groups=groups, tiled=True)]
where the time goes in v6:
time: 44.6 us; the launch traced here: 44.3 us
  blocking collectives  34.9 us (78%)
  starting transfers between devices  3.83 us (9%)
  waiting for transfers between devices  2.36 us (5%)
  Pallas kernels  1.72 us (4%)
  other arithmetic  0.89 us (2%)
  between operations  0.65 us (1%)
    all_to_all x3, blocking collectives, exchange(): lax.all_to_all(chunks, 'f', 0, 0, axis_index_groups=groups, tiled=True)  34.9 us
    ppermute x1, starting transfers between devices, on_device(): far = lax.ppermute(near, 'dp', swap)  3.83 us
    ppermute x1, waiting for transfers between devices, on_device(): far = lax.ppermute(near, 'dp', swap)  2.36 us
    pallas_call x1, Pallas kernels, on_device(): pl.pallas_call(lambda *refs: final_kernel(n_all, f_all, *refs), out_shape...  1.09 us
  transfers between devices with their start and end apart: 1, of which 1 were waited for; matrix products, arithmetic and copies ran while one was open for 0% of the time, Pallas kernels for 0%

profile of v6, /device:TPU:1, one launch (start us, length us, event | category | flops | bytes accessed | tf_op | source)
XLA Modules:
  0.0 44.3 jit_solution(10793996621509694570)
XLA Ops:
  0.6 0.9 %pad_maximum_fusion.refs_1_ = bf16[2,128,256]{2,1,0:T(8,128)(2,1)S(1)} fusion(bf16[1,128,256]{2,1,0:T(8,128)(2,1)} %bitcast.16, bf16[1,128,256]{2,1,0:T(8,128)(2,1)} %bitcast.17), kind=kLoop, calls=%fused_computation | loop fusion | flops 65536 | bytes 262144 | tf_op jit(solution)/shard_map/stack | solution.py:204
  1.5 3.8 %collective-permute-start = (bf16[2,128,256]{2,1,0:T(8,128)(2,1)S(1)}, bf16[2,128,256]{2,1,0:T(8,128)(2,1)S(1)}, u32[]{:S(2)}, u32[]{:S(2)}) collective-permute-start(bf16[2,128,256]{2,1,0:T(8,128)(2,1)S(1)} %pad_maximum_fusion.refs_1_), channel_id=1, source_target_pairs={{0,128},{128,0},{1,129},{129,1},{2,130},{130,2},{3,131},{131,3},{4... | collective-permute-start | bytes 393224 | tf_op jit(solution)/shard_map/ppermute | solution.py:205
  5.3 2.4 %collective-permute-done.refs_2_ = bf16[2,128,256]{2,1,0:T(8,128)(2,1)S(1)} collective-permute-done((bf16[2,128,256]{2,1,0:T(8,128)(2,1)S(1)}, bf16[2,128,256]{2,1,0:T(8,128)(2,1)S(1)}, u32[]{:S(2)}, u32[]{:S(2)}) %collective-permute-start) | collective-permute-done | bytes 131104 | tf_op jit(solution)/shard_map/ppermute | solution.py:205
  7.7 0.5 %gram.1 = (f32[528,128]{1,0:T(8,128)S(1)}, bf16[2,256,256]{2,1,0:T(8,128)(2,1)S(1)}, f32[2,128,256]{2,1,0:T(8,128)S(1)}) custom-call(s32[1]{0:T(128)} %bitcast.refs_0_.place, bf16[2,128,256]{2,1,0:T(8,128)(2,1)S(1)} %pad_maximum_fusion.refs_1_, bf16[2,128,256]{2,1,0:T(8,128)(2,1)S(1)} %collective-permute-done.refs_2_), custom_call_target="tpu_custom_call" | custom-call | tf_op jit(solution)/shard_map/gram/pallas_call | solution.py:207
  8.2 12.7 %all_to_all.15 = f32[16,1,4224]{2,1,0:T(1,128)S(1)} all-to-all(f32[16,1,4224]{2,1,0:T(1,128)S(1)} %bitcast.15), channel_id=1, replica_groups={{81,113,80,65,49,64,112,48,1,97,96,33,32,0,17,16},{83,115,82,67,51,66,1..., dimensions={0} | all-to-all | bytes 540672 | tf_op jit(solution)/shard_map/all_to_all | solution.py:223
  20.9 11.9 %all_to_all.16 = f32[8,1,4224]{2,1,0:T(1,128)S(1)} all-to-all(f32[8,1,4224]{2,1,0:T(1,128)S(1)} %bitcast.13), channel_id=1, replica_groups={{91,93,87,85,83,81,89,95},{123,125,119,117,115,113,121,127},{90,92,86,8..., dimensions={0} | all-to-all | bytes 270336 | tf_op jit(solution)/shard_map/all_to_all | solution.py:223
  32.8 0.1 spread.1
  32.9 10.3 %all_to_all.17 = f32[16,1,3328]{2,1,0:T(1,128)S(1)} all-to-all(f32[16,1,3328]{2,1,0:T(1,128)S(1)} %bitcast.12), channel_id=1, replica_groups={{81,113,80,65,49,64,112,48,1,97,96,33,32,0,17,16},{83,115,82,67,51,66,1..., dimensions={0} | all-to-all | bytes 425984 | tf_op jit(solution)/shard_map/all_to_all | solution.py:223
  43.2 1.1 %final.1 = (f32[128,256]{1,0:T(8,128)}, f32[128,256]{1,0:T(8,128)}, f32[1,1]{1,0:T(1,128)}) custom-call(s32[1]{0:T(128)} %bitcast.refs_0_.place, f32[416,128]{1,0:T(8,128)S(1)} %bitcast.11, bf16[2,256,256]{2,1,0:T(8,128)(2,1)S(1)} %get-tuple-element.10.refs_2_, f32[2,128,256]{2,1,0:T(8,128)S(1)} %get-tuple-element.11.refs_3_), custom_call_target="tpu_custom_call" | custom-call | tf_op jit(solution)/shard_map/final/pallas_call | solution.py:244
  (1 shorter events, 0.0 us)
Async XLA Ops:
  1.5 6.2 %collective-permute-start = (bf16[2,128,256]{2,1,0:T(8,128)(2,1)S(1)}, bf16[2,128,256]{2,1,0:T(8,128)(2,1)S(1)}, u32[]{:S(2)}, u32[]{:S(2)}) collective-permute-start(bf16[2,128,256]{2,1,0:T(8,128)(2,1)S(1)} %pad_maximum_fusion.refs_1_), channel_id=1, source_target_pairs={{0,128},{128,0},{1,129},{129,1},{2,130},{130,2},{3,131},{131,3},{4... | collective-permute-start | bytes 393224 | tf_op jit(solution)/shard_map/ppermute | solution.py:205

commit v7 on v6

--- a/solution.py
+++ b/solution.py
@@ -156,7 +156,7 @@
         pieces.append(total[start + 2 * FOLD : start + PER_VIEW])
     pieces.append(total[DEPTH - 1 :])
     body = total[: DEPTH - 1]
-    pieces.append(jnp.broadcast_to(2.0 * total_sum(body * body), (1, total.shape[1])))
+    pieces.append(2.0 * col_sum(body * body))
     chunk = jnp.concatenate(pieces, axis=0)
     for i in range(spread.shape[0] // OUT_DEPTH):
         spread[i * OUT_DEPTH : (i + 1) * OUT_DEPTH] = chunk
@@ -168,7 +168,7 @@
     first_plane = place[0] == 0
     extra = take_rows(packed, OUT_DEPTH, OUT_DEPTH - 2, 1)
     norms = take_rows(packed, OUT_DEPTH, OUT_DEPTH - 1, 1)
-    square = jnp.sum(norms[:, 0:1], axis=0, keepdims=True)
+    square = total_sum(norms)
     unused, lanes = iotas((1, n_dev))
     for view, grad in enumerate((grad_a, grad_b)):
         folded = take_rows(packed, OUT_DEPTH, view * OUT_VIEW, FOLD)

time: 44.6 us -> 44.5 us (level)
  no operation moved by 1% of the time
where the time goes in v7:
time: 44.5 us; the launch traced here: 44.2 us
  blocking collectives  34.9 us (78%)
  starting transfers between devices  3.83 us (9%)
  waiting for transfers between devices  2.36 us (5%)
  Pallas kernels  1.62 us (4%)
  other arithmetic  0.89 us (2%)
  between operations  0.65 us (1%)
    all_to_all x3, blocking collectives, exchange(): lax.all_to_all(chunks, 'f', 0, 0, axis_index_groups=groups, tiled=True)  34.9 us
    ppermute x1, starting transfers between devices, on_device(): far = lax.ppermute(near, 'dp', swap)  3.83 us
    ppermute x1, waiting for transfers between devices, on_device(): far = lax.ppermute(near, 'dp', swap)  2.36 us
    pallas_call x1, Pallas kernels, on_device(): pl.pallas_call(lambda *refs: final_kernel(n_all, f_all, *refs), out_shape...  1.09 us
  transfers between devices with their start and end apart: 1, of which 1 were waited for; matrix products, arithmetic and copies ran while one was open for 0% of the time, Pallas kernels for 0%

profile of v7, /device:TPU:1, one launch (start us, length us, event | category | flops | bytes accessed | tf_op | source)
XLA Modules:
  0.0 44.2 jit_solution(1412784955456881826)
XLA Ops:
  0.6 0.9 %pad_maximum_fusion.refs_1_ = bf16[2,128,256]{2,1,0:T(8,128)(2,1)S(1)} fusion(bf16[1,128,256]{2,1,0:T(8,128)(2,1)} %bitcast.16, bf16[1,128,256]{2,1,0:T(8,128)(2,1)} %bitcast.17), kind=kLoop, calls=%fused_computation | loop fusion | flops 65536 | bytes 262144 | tf_op jit(solution)/shard_map/stack | solution.py:204
  1.5 3.8 %collective-permute-start = (bf16[2,128,256]{2,1,0:T(8,128)(2,1)S(1)}, bf16[2,128,256]{2,1,0:T(8,128)(2,1)S(1)}, u32[]{:S(2)}, u32[]{:S(2)}) collective-permute-start(bf16[2,128,256]{2,1,0:T(8,128)(2,1)S(1)} %pad_maximum_fusion.refs_1_), channel_id=1, source_target_pairs={{0,128},{128,0},{1,129},{129,1},{2,130},{130,2},{3,131},{131,3},{4... | collective-permute-start | bytes 393224 | tf_op jit(solution)/shard_map/ppermute | solution.py:205
  5.3 2.4 %collective-permute-done.refs_2_ = bf16[2,128,256]{2,1,0:T(8,128)(2,1)S(1)} collective-permute-done((bf16[2,128,256]{2,1,0:T(8,128)(2,1)S(1)}, bf16[2,128,256]{2,1,0:T(8,128)(2,1)S(1)}, u32[]{:S(2)}, u32[]{:S(2)}) %collective-permute-start) | collective-permute-done | bytes 131104 | tf_op jit(solution)/shard_map/ppermute | solution.py:205
  7.7 0.5 %gram.1 = (f32[528,128]{1,0:T(8,128)S(1)}, bf16[2,256,256]{2,1,0:T(8,128)(2,1)S(1)}, f32[2,128,256]{2,1,0:T(8,128)S(1)}) custom-call(s32[1]{0:T(128)} %bitcast.refs_0_.place, bf16[2,128,256]{2,1,0:T(8,128)(2,1)S(1)} %pad_maximum_fusion.refs_1_, bf16[2,128,256]{2,1,0:T(8,128)(2,1)S(1)} %collective-permute-done.refs_2_), custom_call_target="tpu_custom_call" | custom-call | tf_op jit(solution)/shard_map/gram/pallas_call | solution.py:207
  8.2 12.7 %all_to_all.15 = f32[16,1,4224]{2,1,0:T(1,128)S(1)} all-to-all(f32[16,1,4224]{2,1,0:T(1,128)S(1)} %bitcast.15), channel_id=1, replica_groups={{81,113,80,65,49,64,112,48,1,97,96,33,32,0,17,16},{83,115,82,67,51,66,1..., dimensions={0} | all-to-all | bytes 540672 | tf_op jit(solution)/shard_map/all_to_all | solution.py:223
  20.9 11.9 %all_to_all.16 = f32[8,1,4224]{2,1,0:T(1,128)S(1)} all-to-all(f32[8,1,4224]{2,1,0:T(1,128)S(1)} %bitcast.13), channel_id=1, replica_groups={{91,93,87,85,83,81,89,95},{123,125,119,117,115,113,121,127},{90,92,86,8..., dimensions={0} | all-to-all | bytes 270336 | tf_op jit(solution)/shard_map/all_to_all | solution.py:223
  32.8 10.3 %all_to_all.17 = f32[16,1,3328]{2,1,0:T(1,128)S(1)} all-to-all(f32[16,1,3328]{2,1,0:T(1,128)S(1)} %bitcast.12), channel_id=1, replica_groups={{81,113,80,65,49,64,112,48,1,97,96,33,32,0,17,16},{83,115,82,67,51,66,1..., dimensions={0} | all-to-all | bytes 425984 | tf_op jit(solution)/shard_map/all_to_all | solution.py:223
  43.1 1.1 %final.1 = (f32[128,256]{1,0:T(8,128)}, f32[128,256]{1,0:T(8,128)}, f32[1,1]{1,0:T(1,128)}) custom-call(s32[1]{0:T(128)} %bitcast.refs_0_.place, f32[416,128]{1,0:T(8,128)S(1)} %bitcast.11, bf16[2,256,256]{2,1,0:T(8,128)(2,1)S(1)} %get-tuple-element.10.refs_2_, f32[2,128,256]{2,1,0:T(8,128)S(1)} %get-tuple-element.11.refs_3_), custom_call_target="tpu_custom_call" | custom-call | tf_op jit(solution)/shard_map/final/pallas_call | solution.py:244
  (2 shorter events, 0.1 us)
Async XLA Ops:
  1.5 6.2 %collective-permute-start = (bf16[2,128,256]{2,1,0:T(8,128)(2,1)S(1)}, bf16[2,128,256]{2,1,0:T(8,128)(2,1)S(1)}, u32[]{:S(2)}, u32[]{:S(2)}) collective-permute-start(bf16[2,128,256]{2,1,0:T(8,128)(2,1)S(1)} %pad_maximum_fusion.refs_1_), channel_id=1, source_target_pairs={{0,128},{128,0},{1,129},{129,1},{2,130},{130,2},{3,131},{131,3},{4... | collective-permute-start | bytes 393224 | tf_op jit(solution)/shard_map/ppermute | solution.py:205
